TPU v7x, 512 devices: a whole 4x4x16 slice. The times are simulated.
512 devices in a mesh: row: 16 (over z_lo, core), col: 32 (over x, y, z_hi).
Axes of the slice: x: 4, y: 4, z: 16 (z_hi: 2, z_lo: 8; z = z_hi * 8 + z_lo), core: 2. Of those that a mesh axis runs over, the one named last changes fastest.
Arguments:
- greens: float32 [13824, 13824], P('row', 'col')
- accepted_sites: int32 [256], replicated, may hold values from 0 to 13823, as said below
- field_values: int32 [256], replicated, may hold values from -1 to 1, as said below
- left_a: float32 [96, 144, 144], P('row')
- left_b: float32 [96, 144, 144], P('row')
- right_a: float32 [96, 144, 144], P('col')
- right_b: float32 [96, 144, 144], P('col')
Outputs:
- wrapped: float32 [13824, 13824], P('row', 'col')
Inputs may be any that keep to these rules, and one draw needn't show every extreme that they name: `accepted_sites`: site k (from 0) lies in [k * 54, (k + 1) * 54), so the sites rise. `field_values`: each value is -1 or 1.
All inputs are finite; a program needn't handle non-finite values.
Results may differ from a plain program's by a relative error of at most 0.000073.
Values sent between devices are 32-bit elements; how exact they have to be, the bound alone decides.
A program may use at most 64 MiB of HBM per device.

v0:
```python
import jax
import jax.numpy as jnp
from jax import lax
from jax.sharding import PartitionSpec as P

highest = lax.Precision.HIGHEST
coupling = 0.45


def padded_2(x, sides, width):
    for axis, dim in sides:
        size, length = (lax.axis_size(axis), x.shape[dim])
        up = [(i, (i + 1) % size) for i in range(size)]
        down = [(j, i) for i, j in up]
        last = lax.slice_in_dim(x, length - width, length, axis=dim)
        leading = lax.slice_in_dim(x, 0, width, axis=dim)
        before = lax.ppermute(last, axis, up)
        after = lax.ppermute(leading, axis, down)
        x = jnp.concatenate([before, x, after], axis=dim)
    return x


def from_behind(value, axis, steps):
    count = lax.axis_size(axis)
    pairs = [(source, (source + steps) % count) for source in range(count)]
    return lax.ppermute(value, axis, pairs)


def blocks_left(blocks, matrix):
    number = blocks.shape[0]
    cluster = blocks.shape[1]
    product = jnp.einsum(
        "cab,cbm->cam", blocks, matrix.reshape(number, cluster, matrix.shape[1]), precision=highest
    )
    return product.reshape(number * cluster, matrix.shape[1])


def blocks_right(matrix, blocks):
    number = blocks.shape[0]
    cluster = blocks.shape[1]
    product = jnp.einsum(
        "mcb,cba->mca", matrix.reshape(matrix.shape[0], number, cluster), blocks, precision=highest
    )
    return product.reshape(matrix.shape[0], number * cluster)


def left_apply(matrix, first_blocks, second_blocks, carried):
    height = matrix.shape[0]
    margin = first_blocks.shape[1] // 2
    inner = blocks_left(first_blocks, matrix)
    padded = padded_2(inner, (("row", 0),), margin)
    stacked = jnp.concatenate([carried[None], second_blocks], axis=0)
    return blocks_left(stacked, padded)[margin : margin + height]


def right_apply(matrix, first_blocks, second_blocks, carried):
    breadth = matrix.shape[1]
    margin = first_blocks.shape[1] // 2
    inner = blocks_right(matrix, first_blocks)
    padded = padded_2(inner, (("col", 1),), margin)
    stacked = jnp.concatenate([carried[None], second_blocks], axis=0)
    return blocks_right(padded, stacked)[:, margin : margin + breadth]


def whole_apply(matrix, left_a, left_b, right_a, right_b, carried_left, carried_right):
    left_done = left_apply(matrix, left_a, left_b, carried_left)
    return right_apply(left_done, right_a, right_b, carried_right)


def on_device(greens, accepted_sites, field_values, left_a, left_b, right_a, right_b):
    height = greens.shape[0]
    breadth = greens.shape[1]
    accepted = accepted_sites.shape[0]
    row_base = lax.axis_index("row") * height
    col_base = lax.axis_index("col") * breadth
    col_hit = (
        accepted_sites[None, :]
        == col_base + lax.broadcasted_iota(jnp.int32, (breadth, accepted), 0)
    ).astype(jnp.float32)
    row_hit = (
        accepted_sites[:, None] == row_base + lax.broadcasted_iota(jnp.int32, (accepted, height), 1)
    ).astype(jnp.float32)
    g_cols = lax.psum(jnp.dot(greens, col_hit, precision=highest), "col")
    g_rows = lax.psum(jnp.dot(row_hit, greens, precision=highest), "row")
    g_pair = lax.psum(jnp.dot(g_rows, col_hit, precision=highest), "col")
    shifts = jnp.exp(-2.0 * coupling * field_values.astype(jnp.float32)) - 1.0
    identity = jnp.eye(accepted, dtype=jnp.float32)
    capacity = identity + (identity - g_pair) * shifts[None, :]
    normal_matrix = jnp.dot(capacity.T, capacity, precision=highest)
    lower_factor = jnp.linalg.cholesky(normal_matrix)
    middle = lax.linalg.triangular_solve(lower_factor, capacity.T, left_side=True, lower=True)
    inverse = lax.linalg.triangular_solve(
        lower_factor, middle, left_side=True, lower=True, transpose_a=True
    )
    scaled = shifts[:, None] * inverse
    complement = col_hit.T - g_rows
    factor = jnp.dot(scaled, complement, precision=highest)
    carried_left = from_behind(left_b[-1], "row", 1)
    carried_right = from_behind(right_b[-1], "col", 1)
    updated = greens - jnp.dot(g_cols, factor, precision=highest)
    return whole_apply(updated, left_a, left_b, right_a, right_b, carried_left, carried_right)


def solution(mesh):
    return jax.shard_map(
        on_device,
        mesh=mesh,
        in_specs=(
            P("row", "col"),
            P(),
            P(),
            P("row", None, None),
            P("row", None, None),
            P("col", None, None),
            P("col", None, None),
        ),
        out_specs=P("row", "col"),
        check_vma=False,
    )
```

profile of v0, /device:TPU:0, one launch (start us, length us, event | category | flops | bytes accessed | tf_op | source)
XLA Modules:
  0.0 1041.7 jit_solution(11595491443462869906)
XLA Ops:
  6.6 3.4 fusion.4
  10.1 2.1 convolution_bitcast_fusion
  12.2 190.4 %all-reduce.5.cloned.1.call-done = f32[256,432]{0,1:T(8,128)} async-done(((f32[256,432]{0,1:T(8,128)}), f32[256,432]{0,1:T(8,128)}) %all-reduce.5.cloned.1.call-update) | async-done | bytes 442384 | tf_op jit(solution)/shard_map/psum | solution.py:84
  202.5 2.4 fusion.10
  205.0 634.1 %all-reduce.7.cloned.1.call-done = (f32[864,256]{0,1:T(8,128)}, f32[256,256]{1,0:T(8,128)}) async-done(((f32[864,256]{0,1:T(8,128)}, f32[256,256]{1,0:T(8,128)}), (f32[864,256]{0,1:T(8,128)}, f32[256,256]{1,0:T(8,128)})) %all-reduce.7.cloned.1.call-update) | async-done | bytes 1146896 | tf_op jit(solution)/shard_map/psum | solution.py:83
  839.2 1.6 fusion.30
  840.8 1.7 fusion.29
  843.4 11.7 %cholesky.50 = f32[128,128]{1,0:T(8,128)S(1)} custom-call(f32[128,128]{1,0:T(8,128)S(1)} %cholesky.118), custom_call_target="Cholesky" | custom-call | tf_op jit(solution)/shard_map/jit(cholesky)/cholesky | solution.py:90
  855.1 9.8 custom-call.16
  867.1 11.9 %cholesky.105 = f32[128,128]{1,0:T(8,128)S(1)} custom-call(f32[128,128]{1,0:T(8,128)S(1)} %convolution_subtract_fusion.3), custom_call_target="Cholesky" | custom-call | tf_op jit(solution)/shard_map/jit(cholesky)/cholesky | solution.py:90
  881.1 4.0 while.1
  881.8 1.4 bitcast_dynamic-update-slice_fusion.2
  883.8 1.4 bitcast_dynamic-update-slice_fusion.2
  885.1 19.7 %custom-call.17 = f32[2,128,128]{1,2,0:T(8,128)S(1)} custom-call(f32[2,128,128]{2,1,0:T(8,128)S(1)} %get-tuple-element.12), custom_call_target="InvertDiagBlocksLowerTriangular" | custom-call | tf_op jit(solution)/shard_map/triangular_solve | solution.py:92
  904.8 1.3 fusion.31
  906.1 1.3 convolution_subtract_fusion.2
  909.3 2.8 convolution_subtract_fusion
  912.1 2.1 copy.17
  914.2 1.7 fusion.49
  916.0 1.9 collective-permute-start.2
  917.9 10.2 collective-permute-start.3
  928.2 2.1 collective-permute-start.1
  931.0 10.2 collective-permute-done.1
  941.3 1.9 fusion
  943.4 1.7 copy.18
  945.1 3.1 fusion.50
  949.0 14.2 %collective-permute-start.4 = (f32[864,72]{0,1:T(8,128)}, f32[864,72]{0,1:T(8,128)}, u32[]{:S(2)}, u32[]{:S(2)}) collective-permute-start(f32[864,72]{0,1:T(8,128)} %get-tuple-element.27), channel_id=1, source_target_pairs={{0,1},{1,2},{2,3},{3,4},{4,5},{5,6},{6,7},{7,8},{8,9},{9,10},{10,1... | collective-permute-start | bytes 746504 | tf_op jit(solution)/shard_map/ppermute | solution.py:17
  963.2 48.1 %collective-permute-start.5 = (f32[864,72]{0,1:T(8,128)}, f32[864,72]{0,1:T(8,128)}, u32[]{:S(2)}, u32[]{:S(2)}) collective-permute-start(f32[864,72]{0,1:T(8,128)} %get-tuple-element.28), channel_id=1, source_target_pairs={{1,0},{2,1},{3,2},{4,3},{5,4},{6,5},{7,6},{8,7},{9,8},{10,9},{11,1... | collective-permute-start | bytes 746504 | tf_op jit(solution)/shard_map/ppermute | solution.py:18
  1011.6 1.9 collective-permute-start
  1014.0 1.5 collective-permute-done.5
  1016.7 14.9 %collective-permute-done = f32[144,144]{0,1:T(8,128)S(1)} collective-permute-done((f32[144,144]{0,1:T(8,128)S(1)}, f32[144,144]{0,1:T(8,128)S(1)}, u32[]{:S(2)}, u32[]{:S(2)}) %collective-permute-start) | collective-permute-done | bytes 82976 | tf_op jit(solution)/shard_map/ppermute | solution.py:26
  1031.5 2.1 fusion.6
  (61 shorter events, 12.0 us)
Async XLA Ops:
  6.5 907.6 %copy-start = (f32[6,144,144]{2,1,0:T(8,128)S(1)}, f32[6,144,144]{2,1,0:T(8,128)}, u32[]{:S(2)}) copy-start(f32[6,144,144]{2,1,0:T(8,128)} %param.10) | copy-start | bytes 1492996
  6.5 3.5 copy-start.1
  6.5 3.5 copy-start.8
  6.5 196.0 %all-reduce.5.cloned.1.call-start = ((), (), s32[]{:S(2)}) async-start(), calls=%async_computation | async-start | bytes 884736 | tf_op jit(solution)/shard_map/psum | solution.py:84
  10.0 829.2 %all-reduce.7.cloned.1.call-start = ((), (), s32[]{:S(2)}) async-start(), calls=%async_computation.1 | async-start | bytes 2359296 | tf_op jit(solution)/shard_map/psum | solution.py:83
  10.1 194.9 %copy-start.9 = (s32[256]{0:T(256)S(1)}, s32[256]{0:T(256)}, u32[]{:S(2)}) copy-start(s32[256]{0:T(256)} %param.9) | copy-start | bytes 3076
  842.7 0.7 copy-start.5
  881.0 27.6 %copy-start.2 = (f32[256,432]{0,1:T(8,128)S(1)}, f32[256,432]{0,1:T(8,128)}, u32[]{:S(2)}) copy-start(f32[256,432]{0,1:T(8,128)} %all-reduce.5.cloned.1.call-done) | copy-start | bytes 1327108
  904.8 4.5 copy-start.4
  914.2 14.0 %copy-start.3 = (f32[6,144,144]{2,1,0:T(8,128)S(1)}, f32[6,144,144]{2,1,0:T(8,128)}, u32[]{:S(2)}) copy-start(f32[6,144,144]{2,1,0:T(8,128)} %param.11) | copy-start | bytes 1492996
  916.0 14.4 %collective-permute-start.2 = (f32[72,432]{1,0:T(8,128)S(1)}, f32[72,432]{1,0:T(8,128)S(1)}, u32[]{:S(2)}, u32[]{:S(2)}) collective-permute-start(f32[72,432]{1,0:T(8,128)S(1)} %get-tuple-element.25), channel_id=1, source_target_pairs={{0,32},{32,64},{64,96},{96,128},{128,160},{160,192},{192,224},{224... | collective-permute-start | bytes 373256 | tf_op jit(solution)/shard_map/ppermute | solution.py:17
  917.9 12.9 %collective-permute-start.3 = (f32[72,432]{1,0:T(8,128)S(1)}, f32[72,432]{1,0:T(8,128)S(1)}, u32[]{:S(2)}, u32[]{:S(2)}) collective-permute-start(f32[72,432]{1,0:T(8,128)S(1)} %get-tuple-element.26), channel_id=1, source_target_pairs={{32,0},{64,32},{96,64},{128,96},{160,128},{192,160},{224,192},{256... | collective-permute-start | bytes 373256 | tf_op jit(solution)/shard_map/ppermute | solution.py:18
  928.2 13.1 %collective-permute-start.1 = (f32[144,144]{1,0:T(8,128)S(1)}, f32[144,144]{1,0:T(8,128)S(1)}, u32[]{:S(2)}, u32[]{:S(2)}) collective-permute-start(f32[144,144]{1,0:T(8,128)S(1)} %slice_bitcast_fusion.1), channel_id=1, source_target_pairs={{0,32},{32,64},{64,96},{96,128},{128,160},{160,192},{192,224},{224... | collective-permute-start | bytes 248840 | tf_op jit(solution)/shard_map/ppermute | solution.py:26
  943.3 1.7 copy-start.6
  945.1 66.3 %copy-start.7 = (f32[3,144,144]{2,1,0:T(8,128)S(1)}, f32[3,144,144]{2,1,0:T(8,128)}, u32[]{:S(2)}) copy-start(f32[3,144,144]{2,1,0:T(8,128)} %param.13) | copy-start | bytes 746500
  949.0 65.0 %collective-permute-start.4 = (f32[864,72]{0,1:T(8,128)}, f32[864,72]{0,1:T(8,128)}, u32[]{:S(2)}, u32[]{:S(2)}) collective-permute-start(f32[864,72]{0,1:T(8,128)} %get-tuple-element.27), channel_id=1, source_target_pairs={{0,1},{1,2},{2,3},{3,4},{4,5},{5,6},{6,7},{7,8},{8,9},{9,10},{10,1... | collective-permute-start | bytes 746504 | tf_op jit(solution)/shard_map/ppermute | solution.py:17
  963.2 52.2 %collective-permute-start.5 = (f32[864,72]{0,1:T(8,128)}, f32[864,72]{0,1:T(8,128)}, u32[]{:S(2)}, u32[]{:S(2)}) collective-permute-start(f32[864,72]{0,1:T(8,128)} %get-tuple-element.28), channel_id=1, source_target_pairs={{1,0},{2,1},{3,2},{4,3},{5,4},{6,5},{7,6},{8,7},{9,8},{10,9},{11,1... | collective-permute-start | bytes 746504 | tf_op jit(solution)/shard_map/ppermute | solution.py:18
  1011.6 20.0 %collective-permute-start = (f32[144,144]{0,1:T(8,128)S(1)}, f32[144,144]{0,1:T(8,128)S(1)}, u32[]{:S(2)}, u32[]{:S(2)}) collective-permute-start(f32[144,144]{0,1:T(8,128)S(1)} %slice_bitcast_fusion), channel_id=1, source_target_pairs={{0,1},{1,2},{2,3},{3,4},{4,5},{5,6},{6,7},{7,8},{8,9},{9,10},{10,1... | collective-permute-start | bytes 248840 | tf_op jit(solution)/shard_map/ppermute | solution.py:26
Sparse Core Ops, SparseCore 0:
  10.3 192.2 all-reduce.4
  205.8 633.3 all-reduce.6
where the time goes:
time: 1040 us
  waiting for transfers between devices  852 us (82%)
  starting transfers between devices  78.5 us (8%)
  other arithmetic  57 us (5%)
  matrix products  27.8 us (3%)
  between operations  15.1 us (1%)
  local copies, waits for them, and re-layouts  11.1 us (1%)
    psum x1, waiting for transfers between devices, on_device(): g_cols = lax.psum(jnp.dot(greens, col_hit, precision=highest), 'col')  634 us
    psum x1, waiting for transfers between devices, on_device(): g_rows = lax.psum(jnp.dot(row_hit, greens, precision=highest), 'row')  190 us
    ppermute x2, starting transfers between devices, padded_2(): after = lax.ppermute(leading, axis, down)  58.3 us
    another operation x6, other arithmetic, on_device(): lower_factor = jnp.linalg.cholesky(normal_matrix)  34.2 us
    ppermute x2, waiting for transfers between devices, from_behind(): return lax.ppermute(value, axis, pairs)  25.1 us
  transfers between devices with their start and end apart: 8, of which 7 were waited for; matrix products, arithmetic and copies ran while one was open for 0% of the time, Pallas kernels for 0%

commit v1 on v0

v1 whole, which is shorter than its diff:
```python
import functools

import jax
import jax.numpy as jnp
from jax import lax
from jax.experimental import pallas as pl
from jax.experimental.pallas import tpu as pltpu
from jax.sharding import PartitionSpec as P

MESH = pl.DeviceIdType.MESH
f32 = jnp.float32
high = lax.Precision.HIGH
highest = lax.Precision.HIGHEST
coupling = 0.45
series_bound = 1e-7

CS = 144
HALF = 72
ROWS, COLS = 16, 32
HEIGHT, WIDTH = 864, 432
K = 256
KR, KC = 16, 8
WIDE = 512
TALL = 896
EDGE = (0, 128, 768, HEIGHT)


def nn(a, b, precision=high):
    return lax.dot_general(a, b, (((1,), (0,)), ((), ())), precision=precision, preferred_element_type=f32)


def nt(a, b, precision=high):
    return lax.dot_general(a, b, (((1,), (1,)), ((), ())), precision=precision, preferred_element_type=f32)


def iota(shape, dim):
    return lax.broadcasted_iota(jnp.int32, shape, dim)


def exchange_kernel(
    sites, field, g, la, lb, ra, rb,
    acc_out, halo_out, wd_out, norm_out, t_out, u_out, v_out, gp_out,
    q, y, t, acc, qtop, pbot, pb_in, lq_s, lq_in, rq_s, rq_in, redge, redge_t, wd, bloc, rown,
    xs, x_in, edge, ubuf, u, vbuf, gbuf, gp, norm,
    es, er, hs, hr, xsem, xr, cs, cr, vs, vr, us, ur, gs, gr, outs,
):
    r = lax.axis_index("row")
    c = lax.axis_index("col")
    zl, core = r // 2, lax.rem(r, 2)
    zh, xy = lax.rem(c, 2), c // 2
    yy, xx = lax.rem(xy, 4), xy // 4
    rup, rdn = lax.rem(r + 1, ROWS), lax.rem(r + ROWS - 1, ROWS)
    cup, cdn = lax.rem(c + 1, COLS), lax.rem(c + COLS - 1, COLS)
    twin = (r + 1 - 2 * core, c)
    far = (r, c + 1 - 2 * zh)
    ypeer = [(r, (xx * 4 + lax.rem(yy + d, 4)) * 2 + zh) for d in (1, 2, 3)]
    xpeer = [(r, (lax.rem(xx + d, 4) * 4 + yy) * 2 + zh) for d in (1, 2, 3)]
    peers = [(rup, c), (rdn, c), (lax.rem(r + 2, ROWS), c), (lax.rem(r + ROWS - 2, ROWS), c), (r, cup), (r, cdn)]
    peers += ypeer + xpeer
    barrier = pltpu.get_barrier_semaphore()
    for peer in peers:
        pl.semaphore_signal(barrier, inc=1, device_id=peer, device_id_type=MESH)

    def remote(src, dst, send, recv, to):
        return pltpu.make_async_remote_copy(src, dst, send, recv, device_id=to, device_id_type=MESH)

    lane = iota((KR, WIDTH), 1)
    sub = iota((KR, WIDTH), 0)
    rows = jnp.zeros((KR, WIDTH), f32)
    where_site = jnp.full((KR, WIDTH), -1, jnp.int32)
    for j in range(KR):
        site = sites[r * KR + j]
        line = g[pl.ds(jnp.clip(site - r * HEIGHT, 0, HEIGHT - 1), 1), :]
        rows = jnp.where(sub == j, line, rows)
        where_site = jnp.where(sub == j, site - c * WIDTH, where_site)
    x = jnp.where(lane == where_site, 1.0, 0.0) - rows
    hit_lane = iota((128, WIDTH), 1)
    hit_sub = iota((128, WIDTH), 0)
    hit_site = jnp.full((128, WIDTH), -1, jnp.int32)
    for j in range(KC):
        hit_site = jnp.where(hit_sub == 48 + j, sites[c * KC + j] - c * WIDTH, hit_site)
    hit = jnp.where(hit_lane == hit_site, 1.0, 0.0)
    piece = nt(rows, hit, highest)

    redge[...] = jnp.zeros_like(redge)
    lower = jnp.concatenate([jnp.zeros((HALF, CS), f32), rb[2, 0:HALF, :]], axis=0)
    redge[0, 2 * CS : 3 * CS, 0:HALF] = nn(ra[2], lower, highest)[:, HALF:CS]
    redge[1, 0:CS, 0:HALF] = ra[0, :, 0:HALF]
    for d in (0, 1):
        redge_t[d] = redge[d].T[0:HALF, :]
        xs[d] = nn(x, redge[d])
    rq_s[...] = rb[2][HALF:CS, HALF:CS]
    lq_s[...] = lb[5][HALF:CS, HALF:CS]

    for i in range(6):
        q[i * CS : (i + 1) * CS, :] = nn(la[i], g[i * CS : (i + 1) * CS, :])
    pbot[...] = nn(lb[5, HALF:CS, 0:HALF], q[HEIGHT - HALF : HEIGHT, :])
    qtop[...] = q[0:HALF, :]

    pl.semaphore_wait(barrier, len(peers))

    near = [
        remote(xs.at[0], x_in.at[0], xsem.at[0], xr.at[0], (r, cup)),
        remote(xs.at[1], x_in.at[1], xsem.at[1], xr.at[1], (r, cdn)),
        remote(rq_s, rq_in, cs.at[0], cr.at[0], (r, cup)),
        remote(lq_s, lq_in, cs.at[1], cr.at[1], (rup, c)),
        remote(pbot, pb_in.at[0], hs.at[0], hr.at[0], (rup, c)),
        remote(qtop, pb_in.at[1], hs.at[1], hr.at[1], (rdn, c)),
    ]
    for copy in near:
        copy.start()

    for i in range(5):
        y[HALF + i * CS : HALF + (i + 1) * CS, :] = nn(lb[i], q[HALF + i * CS : HALF + (i + 1) * CS, :])

    halos = []

    def send_edge(part):
        lo, hi = EDGE[part], EDGE[part + 1]
        for d, to in ((0, cup), (1, cdn)):
            edge[d, :, lo:hi] = nt(redge_t[d], y[lo:hi, :])
            copy = remote(
                edge.at[d, :, pl.ds(lo, hi - lo)], halo_out.at[d, :, pl.ds(lo, hi - lo)],
                es.at[d, part], er.at[d, part], (r, to),
            )
            copy.start()
            halos.append(copy)

    send_edge(1)
    for copy in near[3:]:
        copy.wait_recv()
    y[0:HALF, :] = pb_in[0] + nn(lq_in[...], q[0:HALF, :])
    y[HEIGHT - HALF : HEIGHT, :] = nn(lb[5, 0:HALF, :], jnp.concatenate([q[HEIGHT - HALF : HEIGHT, :], pb_in[1]], axis=0))
    send_edge(0)
    send_edge(2)

    ubuf[c, :, :] = jnp.zeros((KC, TALL), f32)
    ubuf[c, :, 0:HEIGHT] = nt(hit[48 : 48 + KC, :], y[...])
    u_far = remote(ubuf.at[c], ubuf.at[c], us.at[0], ur.at[0], far)
    u_far.start()

    wd[...] = jnp.zeros_like(wd)
    wd[0:HALF, 0:HALF] = jnp.where(iota((HALF, HALF), 0) == iota((HALF, HALF), 1), 1.0, 0.0)
    wd[HALF:CS, WIDTH - HALF : WIDTH] = rb[2, HALF:CS, 0:HALF]
    bloc[...] = jnp.zeros_like(bloc)
    bloc[HALF : HALF + CS, HALF : HALF + CS] = rb[0]
    bloc[HALF + CS : HALF + 2 * CS, HALF + CS : HALF + 2 * CS] = rb[1]
    bloc[WIDTH - HALF : WIDTH, WIDTH - HALF : WIDTH] = rb[2, 0:HALF, 0:HALF]
    near[2].wait_recv()
    bloc[0:HALF, 0:HALF] = rq_in[...]
    for i in range(3):
        rown[i * CS : (i + 1) * CS, :] = nn(ra[i], bloc[i * CS : (i + 1) * CS, :])

    near[0].wait_recv()
    near[1].wait_recv()
    right = nn(x, rown[...])
    for d in (0, 1):
        right += nn(x_in[d][:, 0:HALF], wd[d * HALF : (d + 1) * HALF, :])
    vbuf[r] = right + jnp.concatenate([jnp.zeros((KR, WIDE - 128), f32), piece], axis=1)

    def slot(j):
        return j * 2 + core

    def chain(j, way):
        to = {0: ((zl + 1) * 2 + core, c), 1: ((zl - 1) * 2 + core, c), 2: twin}[way]
        return remote(vbuf.at[slot(j)], vbuf.at[slot(j)], vs.at[way, j], vr.at[slot(j)], to)

    def arrival(s):
        return remote(vbuf.at[s], vbuf.at[s], vs.at[2, 0], vr.at[s], twin)

    def hand_on(j, way, act):
        go = zl < 7 if way == 0 else zl > 0

        @pl.when(go)
        def _():
            act(chain(j, way))

    start = lambda copy: copy.start()
    hand_on(zl, 0, start)
    hand_on(zl, 1, start)
    chain(zl, 2).start()

    def chain_step(s):
        for way, j, there in ((0, zl - s, zl - s >= 0), (1, zl + s, zl + s <= 7)):

            @pl.when(there)
            def _():
                arrival(slot(j)).wait_recv()
                hand_on(j, way, start)
                chain(j, 2).start()

    def chain_finish():
        for j in range(8):
            arrival(j * 2 + 1 - core).wait_recv()
        hand_on(zl, 0, lambda copy: copy.wait_send())
        hand_on(zl, 1, lambda copy: copy.wait_send())
        chain(zl, 2).wait_send()
        for s in range(1, 8):
            for way, j, there in ((0, zl - s, zl - s >= 0), (1, zl + s, zl + s <= 7)):

                @pl.when(there)
                def _():
                    hand_on(j, way, lambda copy: copy.wait_send())
                    chain(j, 2).wait_send()

    def spread(buf, first, count, send, recv, to):
        ref = buf.at[pl.ds(first, count)]
        return remote(ref, ref, send, recv, to)

    u_y = [spread(ubuf, xy * 2, 2, us.at[1 + d], ur.at[1 + d], ypeer[d]) for d in range(3)]
    u_x = [spread(ubuf, xx * 8, 8, us.at[4 + d], ur.at[4 + d], xpeer[d]) for d in range(3)]
    g_y = [spread(gbuf, xy * 2, 2, gs.at[1 + d], gr.at[1 + d], ypeer[d]) for d in range(3)]
    g_x = [spread(gbuf, xx * 8, 8, gs.at[4 + d], gr.at[4 + d], xpeer[d]) for d in range(3)]
    g_far = remote(gbuf.at[c], gbuf.at[c], gs.at[0], gr.at[0], far)

    u_y_in = [spread(ubuf, (xx * 4 + lax.rem(yy + 3 - d, 4)) * 2, 2, us.at[1 + d], ur.at[1 + d], ypeer[d]) for d in range(3)]
    u_x_in = [spread(ubuf, lax.rem(xx + 3 - d, 4) * 8, 8, us.at[4 + d], ur.at[4 + d], xpeer[d]) for d in range(3)]
    g_y_in = [spread(gbuf, (xx * 4 + lax.rem(yy + 3 - d, 4)) * 2, 2, gs.at[1 + d], gr.at[1 + d], ypeer[d]) for d in range(3)]
    g_x_in = [spread(gbuf, lax.rem(xx + 3 - d, 4) * 8, 8, gs.at[4 + d], gr.at[4 + d], xpeer[d]) for d in range(3)]
    u_far_in = remote(ubuf.at[c + 1 - 2 * zh], ubuf.at[c + 1 - 2 * zh], us.at[0], ur.at[0], far)
    g_far_in = remote(gbuf.at[c + 1 - 2 * zh], gbuf.at[c + 1 - 2 * zh], gs.at[0], gr.at[0], far)

    def rows_of_t(i):
        t[i * CS : (i + 1) * CS, :] = nn(y[i * CS : (i + 1) * CS, :], rown[...][:, 0:WIDTH])

    for s in range(1, 8):
        if s < 7:
            rows_of_t(s - 1)
        if s == 3:
            u_far_in.wait_recv()
            for copy in u_y:
                copy.start()
        if s == 5:
            for copy in u_y_in:
                copy.wait_recv()
            for copy in u_x:
                copy.start()
        chain_step(s)
    chain_finish()

    pieces = vbuf[...].reshape(K, WIDE)[:, WIDE - 128 :]
    gbuf[c] = pieces.T[48 : 48 + KC, :]
    g_far.start()
    outgoing = [pltpu.make_async_copy(t, t_out, outs.at[0]), pltpu.make_async_copy(vbuf, v_out, outs.at[1])]
    outgoing += [pltpu.make_async_copy(wd, wd_out, outs.at[2])]
    for copy in outgoing:
        copy.start()
    g_far_in.wait_recv()
    for copy in g_y:
        copy.start()
    for copy in g_y_in:
        copy.wait_recv()
    for copy in g_x:
        copy.start()
    for copy in u_x_in:
        copy.wait_recv()
    u[...] = ubuf[...].reshape(K, TALL).T
    outgoing.append(pltpu.make_async_copy(u, u_out, outs.at[3]))
    outgoing[-1].start()
    for copy in g_x_in:
        copy.wait_recv()
    gp[...] = gbuf[...].reshape(K, K).T
    outgoing.append(pltpu.make_async_copy(gp, gp_out, outs.at[4]))
    outgoing[-1].start()

    eye = iota((K, K), 0) == iota((K, K), 1)
    shifts = jnp.exp(-2.0 * coupling * field[...].astype(f32)) - 1.0
    pair = gp[...]
    diagonal = jnp.sum(jnp.where(eye, pair, 0.0), axis=0, keepdims=True)
    pivots = 1.0 + (1.0 - diagonal) * shifts
    ratio = shifts / pivots
    ratio_col = jnp.sum(jnp.where(eye, jnp.broadcast_to(ratio, (K, K)), 0.0), axis=1, keepdims=True)
    power = jnp.where(eye, 0.0, pair * ratio)
    z = vbuf[...].reshape(K, WIDE)[:, 0:WIDTH]
    for step in range(4):
        z = z + nn(power, z)
        if step < 3:
            power = nn(power, power)
    total = jnp.sum(jnp.sum(power * power, axis=1, keepdims=True), axis=0, keepdims=True)
    norm[...] = jnp.broadcast_to(total, norm.shape)
    outgoing.append(pltpu.make_async_copy(norm, norm_out, outs.at[5]))
    outgoing[-1].start()
    w = ratio_col * z
    for i in range(6):
        part = slice(i * CS, (i + 1) * CS)
        acc[part, :] = t[part, :] - nn(u[part, :], w)
    outgoing.append(pltpu.make_async_copy(acc, acc_out, outs.at[6]))
    outgoing[-1].start()

    for copy in outgoing:
        copy.wait()
    for copy in near:
        copy.wait_send()
    for copy in [u_far, g_far] + u_y + u_x + g_y + g_x:
        copy.wait_send()
    for copy in halos:
        copy.wait()


def finish_kernel(norm, field, acc, halo, wd, t_hbm, u_hbm, v_hbm, gp_hbm, out, t, u, v, gp, sem):
    edges = halo[...].reshape(2 * HALF, HEIGHT)
    out[...] = acc[...] + lax.dot_general(
        edges, wd[...], (((0,), (0,)), ((), ())), precision=high, preferred_element_type=f32
    )

    @pl.when(jnp.logical_not(norm[0, 0] < series_bound))
    def _():
        for i, (src, dst) in enumerate(((t_hbm, t), (u_hbm, u), (gp_hbm, gp))):
            copy = pltpu.make_async_copy(src, dst, sem.at[i])
            copy.start()
            copy.wait()
        copy = pltpu.make_async_copy(v_hbm, v, sem.at[3])
        copy.start()
        copy.wait()
        eye = iota((K, K), 0) == iota((K, K), 1)
        ident = jnp.where(eye, 1.0, 0.0)
        shifts = jnp.exp(-2.0 * coupling * field[...].astype(f32)) - 1.0
        gp[...] = ident + (ident - gp[...]) * shifts
        index = iota((K, 1), 0)

        def eliminate(k, carry):
            a = gp[...]
            column = jnp.sum(jnp.where(iota((K, K), 1) == k, a, 0.0), axis=1, keepdims=True)
            size = jnp.where(index >= k, jnp.abs(column), -1.0)
            best = jnp.min(jnp.where(size == jnp.max(size), index, K))
            at_k = jnp.sum(jnp.where(index == k, column, 0.0))
            at_best = jnp.sum(jnp.where(index == best, column, 0.0))
            factors = jnp.where(index == best, at_k, column)
            for ref in (gp, v):
                top = ref[pl.ds(best, 1), :] / at_best
                ref[pl.ds(best, 1), :] = ref[pl.ds(k, 1), :]
                ref[...] = jnp.where(index == k, top, ref[...] - factors * top)
            return carry

        lax.fori_loop(0, K, eliminate, 0)
        shift_col = jnp.sum(jnp.where(eye, jnp.broadcast_to(shifts, (K, K)), 0.0), axis=1, keepdims=True)
        w = shift_col * v[...][:, 0:WIDTH]
        fresh = t[...] - nn(u[...][0:HEIGHT, :], w, highest)
        out[...] = fresh + lax.dot_general(
            edges, wd[...], (((0,), (0,)), ((), ())), precision=high, preferred_element_type=f32
        )


def on_device(greens, accepted_sites, field_values, left_a, left_b, right_a, right_b):
    vmem = pl.BlockSpec(memory_space=pltpu.VMEM)
    smem = pl.BlockSpec(memory_space=pltpu.SMEM)
    hbm = pl.BlockSpec(memory_space=pl.ANY)
    shape = lambda *dims: jax.ShapeDtypeStruct(dims, f32)
    v = lambda *dims: pltpu.VMEM(dims, f32)
    dma = lambda *dims: pltpu.SemaphoreType.DMA(dims)
    field = field_values.reshape(1, K)
    acc, halo, wd, norm, t, u, vv, gp = pl.pallas_call(
        exchange_kernel,
        name="exchange",
        out_shape=[
            shape(HEIGHT, WIDTH), shape(2, HALF, HEIGHT), shape(2 * HALF, WIDE), shape(8, 128),
            shape(HEIGHT, WIDTH), shape(TALL, K), shape(ROWS, KR, WIDE), shape(K, K),
        ],
        in_specs=[smem] + [vmem] * 6,
        out_specs=[hbm] * 8,
        scratch_shapes=[
            v(HEIGHT, WIDTH), v(HEIGHT, WIDTH), v(HEIGHT, WIDTH), v(HEIGHT, WIDTH),
            v(HALF, WIDTH), v(HALF, WIDTH), v(2, HALF, WIDTH), v(HALF, HALF), v(HALF, HALF), v(HALF, HALF), v(HALF, HALF),
            v(2, WIDTH, 128), v(2, HALF, WIDTH), v(2 * HALF, WIDE), v(WIDTH, WIDE), v(WIDTH, WIDE),
            v(2, KR, 128), v(2, KR, 128), v(2, HALF, HEIGHT), v(COLS, KC, TALL), v(TALL, K), v(ROWS, KR, WIDE),
            v(COLS, KC, K), v(K, K), v(8, 128),
            dma(2, 3), dma(2, 3), dma(2), dma(2), dma(2), dma(2), dma(2), dma(2), dma(3, 8), dma(16),
            dma(7), dma(7), dma(7), dma(7), dma(7),
        ],
        compiler_params=pltpu.CompilerParams(collective_id=0, has_side_effects=True, vmem_limit_bytes=50 * 2**20),
    )(accepted_sites, field, greens, left_a, left_b, right_a, right_b)
    return pl.pallas_call(
        finish_kernel,
        name="finish",
        out_shape=shape(HEIGHT, WIDTH),
        in_specs=[smem] + [vmem] * 4 + [hbm] * 4,
        out_specs=vmem,
        scratch_shapes=[v(HEIGHT, WIDTH), v(TALL, K), v(K, WIDE), v(K, K), dma(4)],
        compiler_params=pltpu.CompilerParams(vmem_limit_bytes=50 * 2**20),
    )(norm, field, acc, halo, wd[:, 0:WIDTH], t, u, vv.reshape(K, WIDE), gp)


def solution(mesh):
    return jax.shard_map(
        on_device,
        mesh=mesh,
        in_specs=(
            P("row", "col"),
            P(),
            P(),
            P("row", None, None),
            P("row", None, None),
            P("col", None, None),
            P("col", None, None),
        ),
        out_specs=P("row", "col"),
        check_vma=False,
    )
```

time: 1040 us -> 126 us (0.12)
  the two profiles are of different devices: /device:TPU:0 before, /device:TPU:20 now
where the time goes in v1:
time: 126 us; the launch traced here: 125 us
  Pallas kernels  119 us (94%)
  local copies, waits for them, and re-layouts  6.72 us (5%)
    pallas_call x1, Pallas kernels, on_device(): pl.pallas_call(exchange_kernel, name='exchange', out_shape=[shape(HEIGHT,...  115 us
    unnamed x13, local copies, waits for them, and re-layouts  4.09 us
    pallas_call x1, Pallas kernels, on_device(): pl.pallas_call(finish_kernel, name='finish', out_shape=shape(HEIGHT, WIDT...  3.88 us
    pallas_call x1, local copies, waits for them, and re-layouts, on_device(): pl.pallas_call(finish_kernel, name='finish', out_shape=shape(HEIGHT, WIDT...  2.62 us

profile of v1, /device:TPU:20, one launch (start us, length us, event | category | flops | bytes accessed | tf_op | source)
XLA Modules:
  0.0 125.5 jit_solution(10560886236261298703)
XLA Ops:
  0.0 0.0 copy-start.3
  0.0 0.0 copy-start.2
  0.0 0.0 copy-start.1
  0.0 0.0 copy-start.4
  0.0 0.0 copy-start.5
  0.0 2.9 %copy.8.g = f32[864,432]{1,0:T(8,128)} copy(f32[864,432]{0,1:T(8,128)} %param.7) | data formatting | bytes 2985984 | tf_op args[0]
  2.9 0.0 copy-done.3
  2.9 0.0 copy-done.2
  2.9 0.0 copy-done.1
  2.9 0.0 copy-done.4
  3.0 0.0 copy-done.5
  3.0 114.8 %exchange.1 = (f32[864,432]{1,0:T(8,128)}, f32[2,72,864]{2,1,0:T(8,128)S(1)}, f32[144,512]{1,0:T(8,128)S(1)}, f32[8,128]{1,0:T(8,128)S(1)}, f32[864,432]{1,0:T(8...) custom-call(s32[256]{0:T(256)S(1)} %copy-done.5, s32[1,256]{1,0:T(1,128)S(1)} %bitcast.5, ...), custom_call_target="tpu_custom_call" | custom-call | tf_op jit(solution)/shard_map/exchange/pallas_call | solution.py:352
  117.8 0.0 copy-start
  117.8 1.2 copy-done
  119.0 3.9 %finish.1 = f32[864,432]{1,0:T(8,128)} custom-call(f32[8,128]{1,0:T(8,128)S(1)} %get-tuple-element.13.norm, s32[1,256]{1,0:T(1,128)S(1)} %bitcast.6, f32[864,432]{1,0:T(8,128)} %get-tuple-element.14.acc, f32[2,72,864]{2,1,0:T(8,128)S(1)} %get-tuple-element.15.halo, f32[144,432]{1,0:T(8,128)S(1)} %bitcast.4, f32[864,432]{1,0:T(8,128)} %get-tuple-element.17.t_hbm, ...), custom_call_target="tpu_custom_call" | custom-call | tf_op jit(solution)/shard_map/finish/pallas_call | solution.py:372
  122.9 2.6 %copy.9 = f32[864,432]{0,1:T(8,128)} copy(f32[864,432]{1,0:T(8,128)} %finish.1) | data formatting | bytes 2985984 | tf_op jit(solution)/shard_map/finish/pallas_call | solution.py:372
Async XLA Ops:
  0.0 2.9 %copy-start.3 = (f32[3,144,144]{2,1,0:T(8,128)S(1)}, f32[3,144,144]{2,1,0:T(8,128)}, u32[]{:S(2)}) copy-start(f32[3,144,144]{2,1,0:T(8,128)} %rb.1) | copy-start | bytes 746500
  0.0 2.9 %copy-start.2 = (f32[3,144,144]{2,1,0:T(8,128)S(1)}, f32[3,144,144]{2,1,0:T(8,128)}, u32[]{:S(2)}) copy-start(f32[3,144,144]{2,1,0:T(8,128)} %ra.1) | copy-start | bytes 746500
  0.0 2.9 %copy-start.1 = (f32[6,144,144]{2,1,0:T(8,128)S(1)}, f32[6,144,144]{2,1,0:T(8,128)}, u32[]{:S(2)}) copy-start(f32[6,144,144]{2,1,0:T(8,128)} %la.1) | copy-start | bytes 1492996
  0.0 2.9 %copy-start.4 = (s32[256]{0:T(256)S(1)}, s32[256]{0:T(256)}, u32[]{:S(2)}) copy-start(s32[256]{0:T(256)} %param.9) | copy-start | bytes 3076
  0.0 2.9 %copy-start.5 = (s32[256]{0:T(256)S(1)}, s32[256]{0:T(256)}, u32[]{:S(2)}) copy-start(s32[256]{0:T(256)} %sites.1) | copy-start | bytes 3076
  117.8 1.2 copy-start

commit v2 on v0

v2 whole, which is shorter than its diff:
```python
import jax
import jax.numpy as jnp
from jax import lax
from jax.experimental import pallas as pl
from jax.experimental.pallas import tpu as pltpu
from jax.sharding import PartitionSpec as P

MESH = pl.DeviceIdType.MESH
f32 = jnp.float32
high = lax.Precision.HIGH
highest = lax.Precision.HIGHEST
coupling = 0.45
series_bound = 1e-7

CS = 144
HALF = 72
ROWS, COLS = 16, 32
HEIGHT, WIDTH = 864, 432
K = 256
KR, KC = 16, 8
WIDE = 512
TALL = 896
BANDS = ((0, 256, 0, 512), (256, 512, 128, 768), (512, 768, 384, HEIGHT), (768, HEIGHT, 512, HEIGHT))
CHUNKS = 9


def dot(a, b, da, db, precision):
    return lax.dot_general(a, b, (((da,), (db,)), ((), ())), precision=precision, preferred_element_type=f32)


def nn(a, b, precision=high):
    return dot(a, b, 1, 0, precision)


def nt(a, b, precision=high):
    return dot(a, b, 1, 1, precision)


def tn(a, b, precision=high):
    return dot(a, b, 0, 0, precision)


def iota(shape, dim):
    return lax.broadcasted_iota(jnp.int32, shape, dim)


def exchange_kernel(
    sites, field, gt, la, lb, ra, rb,
    acc_out, halo_out, norm_out, t_out, u_out, v_out, gp_out,
    yt, tt, acc, ma, lf, rt, qtop, pbot, top_in, lq_s, lq_in, rq_s, rq_in, redge, redge_t, wd, bloc, rown, rown_t,
    xs, x_in, edge, pbuf, ubuf, vbuf, gbuf, gp, powers, ws, norm,
    es, er, ns, nr, ps, pr, vs, vr, us, ur, gs, gr, outs,
):
    r = lax.axis_index("row")
    c = lax.axis_index("col")
    zl, core = r // 2, lax.rem(r, 2)
    zh, xy = lax.rem(c, 2), c // 2
    yy, xx = lax.rem(xy, 4), xy // 4
    rup, rdn = lax.rem(r + 1, ROWS), lax.rem(r + ROWS - 1, ROWS)
    cup, cdn = lax.rem(c + 1, COLS), lax.rem(c + COLS - 1, COLS)
    twin = (r + 1 - 2 * core, c)
    far_c = c + 1 - 2 * zh
    mates = [(zl // 4) * 4 + lax.rem(lax.rem(zl, 4) + d, 4) for d in (1, 2, 3)]
    across = lax.rem(zl + 4, 8)
    on_line = lambda z: (z * 2 + core, c)
    ypeer = [(r, (xx * 4 + lax.rem(yy + d, 4)) * 2 + zh) for d in (1, 2, 3)]
    xpeer = [(r, (lax.rem(xx + d, 4) * 4 + yy) * 2 + zh) for d in (1, 2, 3)]
    peers = [(rup, c), (rdn, c), (r, cup), (r, cdn), on_line(across)] + [on_line(m) for m in mates] + ypeer + xpeer
    barrier = pltpu.get_barrier_semaphore()
    for peer in peers:
        pl.semaphore_signal(barrier, inc=1, device_id=peer, device_id_type=MESH)

    def remote(src, dst, send, recv, to):
        return pltpu.make_async_remote_copy(src, dst, send, recv, device_id=to, device_id_type=MESH)

    def begin(copies):
        for copy in copies:
            copy.start()

    def arrive(copies):
        for copy in copies:
            copy.wait_recv()

    lane = iota((1, 128), 1)
    row_site = jnp.full((1, 128), -1, jnp.int32)
    for j in range(KR):
        row_site = jnp.where(lane == j, sites[r * KR + j] - r * HEIGHT, row_site)
    rt[...] = nn(gt[...], jnp.where(iota((HEIGHT, 128), 0) == row_site, 1.0, 0.0))
    sub = iota((KR, WIDTH), 0)
    where_site = jnp.full((KR, WIDTH), -1, jnp.int32)
    for j in range(KR):
        where_site = jnp.where(sub == j, sites[r * KR + j] - c * WIDTH, where_site)
    x = jnp.where(iota((KR, WIDTH), 1) == where_site, 1.0, 0.0) - rt[...].T[0:KR, :]
    col_site = [jnp.clip(sites[c * KC + j] - c * WIDTH, 0, WIDTH - 1) for j in range(KC)]

    def site_rows(ref):
        shape = (KC, ref.shape[1])
        out = jnp.zeros(shape, f32)
        for j in range(KC):
            out = jnp.where(iota(shape, 0) == j, ref[pl.ds(col_site[j], 1), :], out)
        return out

    pbuf[r] = site_rows(rt)

    redge[...] = jnp.zeros_like(redge)
    lower = jnp.concatenate([jnp.zeros((HALF, CS), f32), rb[2, 0:HALF, :]], axis=0)
    redge[0, 2 * CS : 3 * CS, 0:HALF] = nn(ra[2], lower, highest)[:, HALF:CS]
    redge[1, 0:CS, 0:HALF] = ra[0, :, 0:HALF]
    for d in (0, 1):
        redge_t[d] = redge[d].T[0:HALF, :]
        xs[d] = nn(x, redge[d])
    rq_s[...] = rb[2][HALF:CS, HALF:CS]
    lq_s[...] = lb[5][HALF:CS, HALF:CS]

    ma[...] = jnp.zeros_like(ma)
    for i in range(6):
        ma[i * CS : (i + 1) * CS, i * CS : (i + 1) * CS] = la[i]
    qtop[...] = nt(gt[:, 0:CS], la[0, 0:HALF, :])
    last = nn(lb[5][HALF:CS, 0:HALF], ma[HEIGHT - HALF : HEIGHT, 640:TALL], highest)
    pbot[...] = nt(gt[:, 640:HEIGHT], last[:, 0 : HEIGHT - 640])

    pl.semaphore_wait(barrier, len(peers))

    near = [
        remote(pbot, top_in.at[0], ns.at[0], nr.at[0], (rup, c)),
        remote(qtop, top_in.at[1], ns.at[1], nr.at[1], (rdn, c)),
        remote(lq_s, lq_in, ns.at[2], nr.at[2], (rup, c)),
        remote(rq_s, rq_in, ns.at[3], nr.at[3], (r, cup)),
        remote(xs.at[0], x_in.at[0], ns.at[4], nr.at[4], (r, cup)),
        remote(xs.at[1], x_in.at[1], ns.at[5], nr.at[5], (r, cdn)),
    ]

    class Tree:
        def __init__(self, buf, send, recv):
            def go(z, i, to):
                ref = buf.at[z * 2 + core]
                return remote(ref, ref, send.at[i], recv.at[z * 2 + core], to)

            def come(s):
                return remote(buf.at[s], buf.at[s], send.at[0], recv.at[s], twin)

            self.first = [go(zl, d, on_line(mates[d])) for d in range(3)]
            self.first += [go(zl, 3, on_line(across)), go(zl, 4, twin)]
            self.across_in = come(across * 2 + core)
            self.second = [go(across, 5 + d, on_line(mates[d])) for d in range(3)] + [go(across, 8, twin)]
            self.mates_in = [come(m * 2 + core) for m in mates]
            self.mates_twin = [go(mates[d], 9 + d, twin) for d in range(3)]
            others = [lax.rem(m + 4, 8) for m in mates]
            self.others_in = [come(m * 2 + core) for m in others]
            self.others_twin = [go(others[d], 12 + d, twin) for d in range(3)]
            self.twins_in = [come(z * 2 + 1 - core) for z in range(8)]
            self.sent = self.first + self.second + self.mates_twin + self.others_twin

        def pass_across(self):
            self.across_in.wait_recv()
            begin(self.second)

        def pass_mates(self):
            for come, go in zip(self.mates_in, self.mates_twin):
                come.wait_recv()
                go.start()

        def pass_others(self):
            for come, go in zip(self.others_in, self.others_twin):
                come.wait_recv()
                go.start()

    p_tree, v_tree = Tree(pbuf, ps, pr), Tree(vbuf, vs, vr)
    begin(p_tree.first)
    begin(near)

    lf[...] = jnp.zeros_like(lf)
    for k in range(5):
        lo, hi = k * CS // 128 * 128, -(-(k + 2) * CS // 128) * 128
        band = slice(HALF + k * CS, HALF + (k + 1) * CS)
        lf[band, lo:hi] = nn(lb[k], ma[band, lo:hi], highest)
    lf[HEIGHT - HALF : HEIGHT, 640:TALL] = nn(lb[5][0:HALF, 0:HALF], ma[HEIGHT - HALF : HEIGHT, 640:TALL], highest)
    p_tree.pass_across()
    for a, b, lo, hi in BANDS:
        yt[:, a:b] = nt(gt[:, lo:hi], lf[a:b, lo:hi])
    p_tree.pass_mates()
    arrive(near[0:3])
    yt[:, 0:HALF] = top_in[0] + nt(qtop[...], lq_in[...])
    tail = jnp.concatenate([jnp.zeros((24, HALF), f32), lb[5][0:HALF, HALF:CS]], axis=0)
    yt[:, 768:HEIGHT] = yt[:, 768:HEIGHT] + nt(top_in[1], tail)
    p_tree.pass_others()

    edge[0] = nn(redge_t[0, :, 256:WIDTH], yt[256:WIDTH, :])
    edge[1] = nn(redge_t[1, :, 0:CS], yt[0:CS, :])
    halos = []
    for k in range(CHUNKS):
        part = pl.ds(k * 8, 8)
        for d, to in ((0, cup), (1, cdn)):
            halos.append(remote(edge.at[d, part], halo_out.at[d, part], es.at[d, k], er.at[d, k], (r, to)))
    poured = [0]

    def pour(n):
        begin(halos[poured[0] * 2 : (poured[0] + n) * 2])
        poured[0] = min(poured[0] + n, CHUNKS)

    class Spread:
        def __init__(self, buf, send, recv):
            def go(first, count, i, to):
                ref = buf.at[pl.ds(first, count)]
                return remote(ref, ref, send.at[i], recv.at[i], to)

            self.far = [go(c, 1, 0, (r, far_c))]
            self.far_in = [go(far_c, 1, 0, (r, far_c))]
            self.y = [go(xy * 2, 2, 1 + d, ypeer[d]) for d in range(3)]
            self.y_in = [go((xx * 4 + lax.rem(yy + 3 - d, 4)) * 2, 2, 1 + d, ypeer[d]) for d in range(3)]
            self.x = [go(xx * 8, 8, 4 + d, xpeer[d]) for d in range(3)]
            self.x_in = [go(lax.rem(xx + 3 - d, 4) * 8, 8, 4 + d, xpeer[d]) for d in range(3)]
            self.sent = self.far + self.y + self.x

    u_spread, g_spread = Spread(ubuf, us, ur), Spread(gbuf, gs, gr)
    ubuf[c] = site_rows(yt)
    begin(u_spread.far)
    pour(1)

    arrive(p_tree.twins_in)
    halves = []
    for h in (0, 1):
        half = pbuf[8 * h]
        for j in range(1, 8):
            half = half + pltpu.roll(pbuf[8 * h + j], 16 * j, 1)
        halves.append(half)
    gbuf[c] = jnp.concatenate(halves, axis=1)
    begin(g_spread.far)

    bloc[...] = jnp.zeros_like(bloc)
    bloc[HALF : HALF + CS, HALF : HALF + CS] = rb[0]
    bloc[HALF + CS : HALF + 2 * CS, HALF + CS : HALF + 2 * CS] = rb[1]
    bloc[WIDTH - HALF : WIDTH, WIDTH - HALF : WIDTH] = rb[2, 0:HALF, 0:HALF]
    wd[...] = jnp.zeros_like(wd)
    wd[:, WIDTH - HALF : WIDTH] = rb[2, HALF:CS, 0:HALF]
    near[3].wait_recv()
    bloc[0:HALF, 0:HALF] = rq_in[...]
    for i in range(3):
        rown[i * CS : (i + 1) * CS, :] = nn(ra[i], bloc[i * CS : (i + 1) * CS, :], highest)
    arrive(near[4:6])
    right = nn(x, rown[...]) + nn(x_in[1][:, 0:HALF], wd[...])
    vbuf[r] = right[:, 0:WIDTH] + jnp.concatenate([x_in[0], jnp.zeros((KR, WIDTH - 128), f32)], axis=1)
    begin(v_tree.first)
    pour(1)
    rown_t[...] = rown[...].T[0:WIDTH, :]

    def rows_of_t(i):
        part = slice(i * CS, (i + 1) * CS)
        tt[part, :] = nn(rown_t[part, :], yt[...])

    arrive(g_spread.far_in)
    begin(g_spread.y)
    v_tree.pass_across()
    arrive(u_spread.far_in)
    begin(u_spread.y)
    pour(1)
    rows_of_t(0)
    arrive(g_spread.y_in)
    begin(g_spread.x)
    v_tree.pass_mates()
    arrive(u_spread.y_in)
    begin(u_spread.x)
    pour(2)
    rows_of_t(1)
    v_tree.pass_others()
    pour(CHUNKS)
    rows_of_t(2)
    outgoing = [pltpu.make_async_copy(tt, t_out, outs.at[0])]
    outgoing[-1].start()

    arrive(g_spread.x_in)
    gp[...] = gbuf[...].reshape(K, K).T
    outgoing.append(pltpu.make_async_copy(gp, gp_out, outs.at[1]))
    outgoing[-1].start()
    eye = iota((K, K), 0) == iota((K, K), 1)
    shifts = jnp.exp(-2.0 * coupling * field[...].astype(f32)) - 1.0
    pair = gp[...]
    diagonal = jnp.sum(jnp.where(eye, pair, 0.0), axis=0, keepdims=True)
    ratio = shifts / (1.0 + (1.0 - diagonal) * shifts)
    ratio_col = jnp.sum(jnp.where(eye, jnp.broadcast_to(ratio, (K, K)), 0.0), axis=1, keepdims=True)
    powers[0] = jnp.where(eye, 0.0, pair * ratio)
    for step in range(3):
        powers[step + 1] = nn(powers[step], powers[step])
    total = jnp.sum(jnp.sum(powers[3] * powers[3], axis=1, keepdims=True), axis=0, keepdims=True)
    norm[...] = jnp.broadcast_to(total, norm.shape)
    outgoing.append(pltpu.make_async_copy(norm, norm_out, outs.at[2]))
    outgoing[-1].start()

    arrive(v_tree.twins_in)
    outgoing.append(pltpu.make_async_copy(vbuf, v_out, outs.at[3]))
    outgoing[-1].start()
    z = vbuf[...].reshape(K, WIDTH)
    for step in range(4):
        z = z + nn(powers[step], z)
    ws[...] = jnp.zeros_like(ws)
    ws[:, 0:WIDTH] = ratio_col * z
    wt = ws[...].T
    arrive(u_spread.x_in)
    outgoing.append(pltpu.make_async_copy(ubuf, u_out, outs.at[4]))
    outgoing[-1].start()
    for i in range(3):
        part = slice(i * CS, (i + 1) * CS)
        acc[part, :] = tt[part, :] - nn(wt[part, :], ubuf[...].reshape(K, HEIGHT))
    outgoing.append(pltpu.make_async_copy(acc, acc_out, outs.at[5]))
    outgoing[-1].start()

    for copy in outgoing:
        copy.wait()
    for copy in near + p_tree.sent + v_tree.sent + u_spread.sent + g_spread.sent:
        copy.wait_send()
    for copy in halos:
        copy.wait()


def finish_kernel(norm, field, halo, rb, acc_hbm, t_hbm, u_hbm, v_hbm, gp_hbm, out_hbm, low, top, t, u, v, gp, sem):
    inner = pl.ds(HALF, WIDTH - 2 * HALF)
    first, final = pl.ds(0, HALF), pl.ds(WIDTH - HALF, HALF)
    middle = pltpu.make_async_copy(acc_hbm.at[inner], out_hbm.at[inner], sem.at[0])
    loads = [pltpu.make_async_copy(acc_hbm.at[first], low, sem.at[1]), pltpu.make_async_copy(acc_hbm.at[final], top, sem.at[2])]
    stores = [pltpu.make_async_copy(low, out_hbm.at[first], sem.at[1]), pltpu.make_async_copy(top, out_hbm.at[final], sem.at[2])]
    middle.start()
    for copy in loads:
        copy.start()
    above = tn(rb[2][HALF:CS, 0:HALF], halo[1])
    loads[0].wait()
    low[...] = low[...] + halo[0]
    stores[0].start()
    loads[1].wait()
    top[...] = top[...] + above
    stores[1].start()
    middle.wait()
    for copy in stores:
        copy.wait()

    @pl.when(jnp.logical_not(norm[0, 0] < series_bound))
    def _():
        for i, (src, dst) in enumerate(((t_hbm, t), (u_hbm, u), (v_hbm, v), (gp_hbm, gp))):
            copy = pltpu.make_async_copy(src, dst, sem.at[i])
            copy.start()
            copy.wait()
        eye = iota((K, K), 0) == iota((K, K), 1)
        ident = jnp.where(eye, 1.0, 0.0)
        shifts = jnp.exp(-2.0 * coupling * field[...].astype(f32)) - 1.0
        gp[...] = ident + (ident - gp[...]) * shifts
        index = iota((K, 1), 0)

        def eliminate(k, carry):
            a = gp[...]
            column = jnp.sum(jnp.where(iota((K, K), 1) == k, a, 0.0), axis=1, keepdims=True)
            size = jnp.where(index >= k, jnp.abs(column), -1.0)
            best = jnp.min(jnp.where(size == jnp.max(size), index, K - 1))
            at_k = jnp.sum(jnp.where(index == k, column, 0.0))
            at_best = jnp.sum(jnp.where(index == best, column, 0.0))
            factors = jnp.where(index == best, at_k, column)
            for ref in (gp, v):
                line = ref[pl.ds(best, 1), :] / at_best
                ref[pl.ds(best, 1), :] = ref[pl.ds(k, 1), :]
                ref[...] = jnp.where(index == k, line, ref[...] - factors * line)
            return carry

        lax.fori_loop(0, K, eliminate, 0)
        shift_col = jnp.sum(jnp.where(eye, jnp.broadcast_to(shifts, (K, K)), 0.0), axis=1, keepdims=True)
        t[...] = t[...] - tn(shift_col * v[...], u[...], highest)
        t[0:HALF, :] = t[0:HALF, :] + halo[0]
        t[WIDTH - HALF : WIDTH, :] = t[WIDTH - HALF : WIDTH, :] + above
        copy = pltpu.make_async_copy(t, out_hbm, sem.at[0])
        copy.start()
        copy.wait()


def on_device(greens, accepted_sites, field_values, left_a, left_b, right_a, right_b):
    vmem = pl.BlockSpec(memory_space=pltpu.VMEM)
    smem = pl.BlockSpec(memory_space=pltpu.SMEM)
    hbm = pl.BlockSpec(memory_space=pltpu.HBM)
    shape = lambda *dims: jax.ShapeDtypeStruct(dims, f32)
    v = lambda *dims: pltpu.VMEM(dims, f32)
    dma = lambda *dims: pltpu.SemaphoreType.DMA(dims)
    field = field_values.reshape(1, K)
    acc, halo, norm, t, u, vv, gp = pl.pallas_call(
        exchange_kernel,
        name="exchange",
        out_shape=[
            shape(WIDTH, HEIGHT), shape(2, HALF, HEIGHT), shape(8, 128),
            shape(WIDTH, HEIGHT), shape(COLS, KC, HEIGHT), shape(ROWS, KR, WIDTH), shape(K, K),
        ],
        in_specs=[smem] + [vmem] * 6,
        out_specs=[hbm] * 7,
        scratch_shapes=[
            v(WIDTH, HEIGHT), v(WIDTH, HEIGHT), v(WIDTH, HEIGHT), v(HEIGHT, TALL), v(HEIGHT, TALL), v(WIDTH, 128),
            v(WIDTH, HALF), v(WIDTH, HALF), v(2, WIDTH, HALF), v(HALF, HALF), v(HALF, HALF), v(HALF, HALF), v(HALF, HALF),
            v(2, WIDTH, 128), v(2, HALF, WIDTH), v(HALF, WIDE), v(WIDTH, WIDE), v(WIDTH, WIDE), v(WIDTH, WIDTH),
            v(2, KR, 128), v(2, KR, 128), v(2, HALF, HEIGHT), v(ROWS, KC, 128), v(COLS, KC, HEIGHT), v(ROWS, KR, WIDTH),
            v(COLS, KC, K), v(K, K), v(4, K, K), v(K, WIDE), v(8, 128),
            dma(2, CHUNKS), dma(2, CHUNKS), dma(6), dma(6), dma(15), dma(16), dma(15), dma(16),
            dma(7), dma(7), dma(7), dma(7), dma(6),
        ],
        compiler_params=pltpu.CompilerParams(collective_id=0, has_side_effects=True, vmem_limit_bytes=50 * 2**20),
    )(accepted_sites, field, greens.T, left_a, left_b, right_a, right_b)
    out = pl.pallas_call(
        finish_kernel,
        name="finish",
        out_shape=shape(WIDTH, HEIGHT),
        in_specs=[smem] + [vmem] * 3 + [hbm] * 5,
        out_specs=hbm,
        scratch_shapes=[
            v(HALF, HEIGHT), v(HALF, HEIGHT), v(WIDTH, HEIGHT), v(K, HEIGHT), v(K, WIDTH), v(K, K), dma(4),
        ],
        compiler_params=pltpu.CompilerParams(vmem_limit_bytes=50 * 2**20),
    )(norm, field, halo, right_b, acc, t, u.reshape(K, HEIGHT), vv.reshape(K, WIDTH), gp)
    return out.T


def solution(mesh):
    return jax.shard_map(
        on_device,
        mesh=mesh,
        in_specs=(
            P("row", "col"),
            P(),
            P(),
            P("row", None, None),
            P("row", None, None),
            P("col", None, None),
            P("col", None, None),
        ),
        out_specs=P("row", "col"),
        check_vma=False,
    )
```

time: 1040 us -> 146 us (0.14)
  the two profiles are of different devices: /device:TPU:0 before, /device:TPU:3 now
where the time goes in v2:
time: 146 us
  Pallas kernels  139 us (95%)
  local copies, waits for them, and re-layouts  6.89 us (5%)
    pallas_call x1, Pallas kernels, on_device(): pl.pallas_call(exchange_kernel, name='exchange', out_shape=[shape(WIDTH,...  106 us
    pallas_call x1, Pallas kernels, on_device(): pl.pallas_call(finish_kernel, name='finish', out_shape=shape(WIDTH, HEIGH...  33 us
    unnamed x16, local copies, waits for them, and re-layouts  6.89 us

profile of v2, /device:TPU:3, one launch (start us, length us, event | category | flops | bytes accessed | tf_op | source)
XLA Modules:
  0.0 146.1 jit_solution(9409548650722702662)
XLA Ops:
  0.0 0.0 copy-start
  0.0 1.0 copy-done
  1.0 0.0 copy-start.3
  1.0 1.2 copy-done.3
  2.2 0.0 copy-start.4
  2.2 1.2 copy-done.4
  3.4 0.0 copy-start.5
  3.4 1.0 copy-done.5
  4.4 0.0 copy-start.6
  4.4 0.7 copy-done.6
  5.0 0.0 copy-start.7
  5.0 0.7 copy-done.7
  5.7 0.0 copy-start.1
  5.7 106.0 %exchange.1 = (f32[432,864]{1,0:T(8,128)}, f32[2,72,864]{2,1,0:T(8,128)S(1)}, f32[8,128]{1,0:T(8,128)S(1)}, f32[432,864]{1,0:T(8,128)}, f32[32,8,864]{2,1,0:T(8,...) custom-call(s32[256]{0:T(256)S(1)} %copy-done.7, s32[1,256]{1,0:T(1,128)S(1)} %bitcast.7, f32[432,864]{1,0:T(8,128)} %bitcast.9, ...), custom_call_target="tpu_custom_call" | custom-call | tf_op jit(solution)/shard_map/exchange/pallas_call | solution.py:379
  111.7 0.0 copy-done.1
  111.7 0.0 copy-start.2
  111.8 1.2 copy-done.2
  112.9 33.0 %finish.1 = f32[432,864]{1,0:T(8,128)} custom-call(f32[8,128]{1,0:T(8,128)S(1)} %get-tuple-element.12.norm, s32[1,256]{1,0:T(1,128)S(1)} %bitcast.8, f32[2,72,864]{2,1,0:T(8,128)S(1)} %get-tuple-element.13.halo, f32[3,144,144]{2,1,0:T(8,128)S(1)} %copy-done.1, f32[432,864]{1,0:T(8,128)} %get-tuple-element.14.acc_hbm, f32[432,864]{1,0:T(8,128)} %get-tuple-element.15.t_hbm, ...), custom_call_target="tpu_custom_call" | custom-call | tf_op jit(solution)/shard_map/finish/pallas_call | solution.py:399
Async XLA Ops:
  0.0 1.0 copy-start
  1.0 1.2 copy-start.3
  2.2 1.2 copy-start.4
  3.4 1.0 copy-start.5
  4.4 0.7 copy-start.6
  5.0 0.7 copy-start.7
  5.7 106.0 %copy-start.1 = (f32[3,144,144]{2,1,0:T(8,128)S(1)}, f32[3,144,144]{2,1,0:T(8,128)}, u32[]{:S(2)}) copy-start(f32[3,144,144]{2,1,0:T(8,128)} %rb.3) | copy-start | bytes 746500
  111.7 1.2 copy-start.2

commit v3 on v2

v3 whole, which is shorter than its diff:
```python
import jax
import jax.numpy as jnp
from jax import lax
from jax.experimental import pallas as pl
from jax.experimental.pallas import tpu as pltpu
from jax.sharding import PartitionSpec as P

MESH = pl.DeviceIdType.MESH
f32 = jnp.float32
high = lax.Precision.HIGH
highest = lax.Precision.HIGHEST
coupling = 0.45
series_bound = 1e-7

CS = 144
HALF = 72
ROWS, COLS = 16, 32
HEIGHT, WIDTH = 864, 432
K = 256
KR, KC = 16, 8
WIDE = 512
TALL = 896
BANDS = ((0, 256, 0, 512), (256, 512, 128, 768), (512, 768, 384, HEIGHT), (768, HEIGHT, 512, HEIGHT))
CHUNKS = 9
POUR = (9, 0, 0, 9)


def dot(a, b, da, db, precision):
    return lax.dot_general(a, b, (((da,), (db,)), ((), ())), precision=precision, preferred_element_type=f32)


def nn(a, b, precision=high):
    return dot(a, b, 1, 0, precision)


def nt(a, b, precision=high):
    return dot(a, b, 1, 1, precision)


def tn(a, b, precision=high):
    return dot(a, b, 0, 0, precision)


def iota(shape, dim):
    return lax.broadcasted_iota(jnp.int32, shape, dim)


def exchange_kernel(
    sites_hbm, field_hbm, gt_hbm, la_hbm, lb_hbm, ra_hbm, rb_hbm,
    acc_out, halo_out, norm_out, mix_out, t_out, u_out, v_out, gp_out,
    sites, field, gt, la, lb, ra, rb, yt, tt, acc, ma, lf, rt, qtop, pbot, top_in, lq_s, lq_in, rq_s, rq_in, redge, redge_t, wd, bloc, rown, rown_t,
    xs, x_in, edge, pbuf, ubuf, vbuf, vall, gbuf, gp, powers, ws, norm, mix,
    es, er, ns, nr, ps, pr, vs, vr, us, ur, gs, gr, ins, outs,
):
    r = lax.axis_index("row")
    c = lax.axis_index("col")
    zl, core = r // 2, lax.rem(r, 2)
    zh, xy = lax.rem(c, 2), c // 2
    yy, xx = lax.rem(xy, 4), xy // 4
    rup, rdn = lax.rem(r + 1, ROWS), lax.rem(r + ROWS - 1, ROWS)
    cup, cdn = lax.rem(c + 1, COLS), lax.rem(c + COLS - 1, COLS)
    twin = (r + 1 - 2 * core, c)
    far_c = c + 1 - 2 * zh
    on_line = lambda z: (z * 2 + core, c)
    ypeer = [(r, (xx * 4 + lax.rem(yy + d, 4)) * 2 + zh) for d in (1, 2, 3)]
    xpeer = [(r, (lax.rem(xx + d, 4) * 4 + yy) * 2 + zh) for d in (1, 2, 3)]
    zf = zh * 8 + zl
    ring = [lax.rem(zf + d, 16) for d in range(1, 16)]
    on_ring = lambda z: (lax.rem(z, 8) * 2 + core, xy * 2 + z // 8)
    peers = [(rup, c), (rdn, c), (r, cup), (r, cdn)] + [on_ring(z) for z in ring] + ypeer + xpeer
    barrier = pltpu.get_barrier_semaphore()
    for peer in peers:
        pl.semaphore_signal(barrier, inc=1, device_id=peer, device_id_type=MESH)
    pairs = ((sites_hbm, sites), (gt_hbm, gt), (ra_hbm, ra), (rb_hbm, rb), (la_hbm, la), (lb_hbm, lb), (field_hbm, field))
    loads = [pltpu.make_async_copy(src, dst, ins.at[i]) for i, (src, dst) in enumerate(pairs)]
    for load in loads:
        load.start()
    redge[...] = jnp.zeros_like(redge)
    ma[...] = jnp.zeros_like(ma)
    lf[...] = jnp.zeros_like(lf)
    loads[0].wait()

    def remote(src, dst, send, recv, to):
        return pltpu.make_async_remote_copy(src, dst, send, recv, device_id=to, device_id_type=MESH)

    def begin(copies):
        for copy in copies:
            copy.start()

    def arrive(copies):
        for copy in copies:
            copy.wait_recv()

    lane = iota((1, 128), 1)
    row_site = jnp.full((1, 128), -1, jnp.int32)
    for j in range(KR):
        row_site = jnp.where(lane == j, sites[r * KR + j] - r * HEIGHT, row_site)
    loads[1].wait()
    rt[...] = nn(gt[...], jnp.where(iota((HEIGHT, 128), 0) == row_site, 1.0, 0.0))
    sub = iota((KR, WIDTH), 0)
    where_site = jnp.full((KR, WIDTH), -1, jnp.int32)
    for j in range(KR):
        where_site = jnp.where(sub == j, sites[r * KR + j] - c * WIDTH, where_site)
    x = jnp.where(iota((KR, WIDTH), 1) == where_site, 1.0, 0.0) - rt[...].T[0:KR, :]
    col_site = [jnp.clip(sites[c * KC + j] - c * WIDTH, 0, WIDTH - 1) for j in range(KC)]

    def site_rows(ref):
        shape = (KC, ref.shape[1])
        out = jnp.zeros(shape, f32)
        for j in range(KC):
            out = jnp.where(iota(shape, 0) == j, ref[pl.ds(col_site[j], 1), :], out)
        return out

    pbuf[core, zf] = site_rows(rt)

    loads[2].wait()
    loads[3].wait()
    lower = jnp.concatenate([jnp.zeros((HALF, CS), f32), rb[2, 0:HALF, :]], axis=0)
    redge[0, 2 * CS : 3 * CS, 0:HALF] = nn(ra[2], lower, highest)[:, HALF:CS]
    redge[1, 0:CS, 0:HALF] = ra[0, :, 0:HALF]
    for d in (0, 1):
        redge_t[d] = redge[d].T[0:HALF, :]
        xs[d] = nn(x, redge[d])
    rq_s[...] = rb[2][HALF:CS, HALF:CS]

    pl.semaphore_wait(barrier, len(peers))

    far = [
        remote(xs.at[0], x_in.at[0], ns.at[4], nr.at[4], (r, cup)),
        remote(xs.at[1], x_in.at[1], ns.at[5], nr.at[5], (r, cdn)),
        remote(rq_s, rq_in, ns.at[3], nr.at[3], (r, cup)),
    ]
    begin(far)
    pieces = [remote(pbuf.at[core, zf], pbuf.at[core, zf], ps.at[d], pr.at[zf], on_ring(ring[d])) for d in range(15)]
    pieces_in = [remote(pbuf.at[core, z], pbuf.at[core, z], ps.at[0], pr.at[z], twin) for z in ring]
    pieces_twin = remote(pbuf.at[core], pbuf.at[core], ps.at[15], pr.at[16], twin)
    pieces_twin_in = remote(pbuf.at[1 - core], pbuf.at[1 - core], ps.at[15], pr.at[16], twin)
    begin(pieces)

    mix[...] = rb[2][HALF:CS, 0:HALF]
    outgoing = [pltpu.make_async_copy(mix, mix_out, outs.at[8])]
    outgoing[-1].start()
    loads[4].wait()
    loads[5].wait()
    loads[6].wait()
    lq_s[...] = lb[5][HALF:CS, HALF:CS]

    for i in range(6):
        ma[i * CS : (i + 1) * CS, i * CS : (i + 1) * CS] = la[i]
    qtop[...] = nt(la[0, 0:HALF, :], gt[:, 0:CS])
    last = nn(lb[5][HALF:CS, 0:HALF], ma[HEIGHT - HALF : HEIGHT, 640:TALL], highest)
    pbot[...] = nt(last[:, 0 : HEIGHT - 640], gt[:, 640:HEIGHT])

    near = [
        remote(pbot, top_in.at[0], ns.at[0], nr.at[0], (rup, c)),
        remote(qtop, top_in.at[1], ns.at[1], nr.at[1], (rdn, c)),
        remote(lq_s, lq_in, ns.at[2], nr.at[2], (rup, c)),
    ]
    begin(near)

    others = [lax.rem(zl + d, 8) for d in range(1, 8)]
    rows_out = [remote(vbuf.at[core, zl], vbuf.at[core, zl], vs.at[d], vr.at[zl], on_line(others[d])) for d in range(7)]
    rows_in = [remote(vbuf.at[core, z], vbuf.at[core, z], vs.at[0], vr.at[z], twin) for z in others]
    rows_twin = remote(vbuf.at[core], vbuf.at[core], vs.at[7], vr.at[8], twin)
    rows_twin_in = remote(vbuf.at[1 - core], vbuf.at[1 - core], vs.at[7], vr.at[8], twin)

    for k in range(5):
        lo, hi = k * CS // 128 * 128, -(-(k + 2) * CS // 128) * 128
        band = slice(HALF + k * CS, HALF + (k + 1) * CS)
        lf[band, lo:hi] = nn(lb[k], ma[band, lo:hi], highest)
    lf[HEIGHT - HALF : HEIGHT, 640:TALL] = nn(lb[5][0:HALF, 0:HALF], ma[HEIGHT - HALF : HEIGHT, 640:TALL], highest)
    bloc[...] = jnp.zeros_like(bloc)
    bloc[HALF : HALF + CS, HALF : HALF + CS] = rb[0]
    bloc[HALF + CS : HALF + 2 * CS, HALF + CS : HALF + 2 * CS] = rb[1]
    bloc[WIDTH - HALF : WIDTH, WIDTH - HALF : WIDTH] = rb[2, 0:HALF, 0:HALF]
    wd[...] = jnp.zeros_like(wd)
    wd[:, WIDTH - HALF : WIDTH] = rb[2, HALF:CS, 0:HALF]
    for i in range(3):
        rown[i * CS : (i + 1) * CS, :] = nn(ra[i], bloc[i * CS : (i + 1) * CS, :], highest)
    right = nn(x, rown[...])
    for a, b, lo, hi in BANDS:
        yt[:, a:b] = nt(gt[:, lo:hi], lf[a:b, lo:hi])
    arrive(far)
    first = x_in[0] + jnp.concatenate([nn(xs[1][:, 0:HALF], rq_in[...]), jnp.zeros((KR, 128 - HALF), f32)], axis=1)
    right += nn(x_in[1][:, 0:HALF], wd[...])
    vbuf[core, zl] = right[:, 0:WIDTH] + jnp.concatenate([first, jnp.zeros((KR, WIDTH - 128), f32)], axis=1)
    begin(rows_out)
    arrive(near)
    one = jnp.where(iota((HALF, HALF), 0) == iota((HALF, HALF), 1), 1.0, 0.0)
    yt[:, 0:HALF] = tn(jnp.concatenate([top_in[0], nn(lq_in[...], qtop[...])], axis=0), jnp.concatenate([one, one], axis=0))
    tail = jnp.concatenate([jnp.zeros((24, HALF), f32), lb[5][0:HALF, HALF:CS]], axis=0)
    yt[:, 768:HEIGHT] = yt[:, 768:HEIGHT] + tn(top_in[1], tail.T)

    edge[0] = nn(redge_t[0, :, 256:WIDTH], yt[256:WIDTH, :])
    edge[1] = nn(redge_t[1, :, 0:CS], yt[0:CS, :])
    halos = []
    for k in range(CHUNKS):
        part = pl.ds(k * 8, 8)
        for d, to in ((0, cup), (1, cdn)):
            halos.append(remote(edge.at[d, part], halo_out.at[d, part], es.at[d, k], er.at[d, k], (r, to)))
    poured = [0]

    def pour(n):
        begin(halos[poured[0] * 2 : (poured[0] + n) * 2])
        poured[0] = min(poured[0] + n, CHUNKS)

    class Spread:
        def __init__(self, buf, send, recv):
            def go(first, count, i, to):
                ref = buf.at[pl.ds(first, count)]
                return remote(ref, ref, send.at[i], recv.at[i], to)

            self.far = [go(c, 1, 0, (r, far_c))]
            self.far_in = [go(far_c, 1, 0, (r, far_c))]
            self.y = [go(xy * 2, 2, 1 + d, ypeer[d]) for d in range(3)]
            self.y_in = [go((xx * 4 + lax.rem(yy + 3 - d, 4)) * 2, 2, 1 + d, ypeer[d]) for d in range(3)]
            self.x = [go(xx * 8, 8, 4 + d, xpeer[d]) for d in range(3)]
            self.x_in = [go(lax.rem(xx + 3 - d, 4) * 8, 8, 4 + d, xpeer[d]) for d in range(3)]
            self.sent = self.far + self.y + self.x

    u_spread, g_spread = Spread(ubuf, us, ur), Spread(gbuf, gs, gr)
    ubuf[c] = site_rows(yt)
    begin(u_spread.far)
    pour(POUR[0])

    arrive(pieces_in)
    pieces_twin.start()
    pour(POUR[1])
    pieces_twin_in.wait_recv()
    for side in (0, 1):
        halves = []
        for h in (0, 1):
            half = pbuf[0, side * 8 + 4 * h]
            for j in range(1, 8):
                half = half + pltpu.roll(pbuf[j % 2, side * 8 + 4 * h + j // 2], 16 * j, 1)
            halves.append(half)
        gbuf[xy * 2 + side] = jnp.concatenate(halves, axis=1)
    begin(g_spread.y)
    pour(POUR[2])
    rown_t[...] = rown[...].T[0:WIDTH, :]

    def rows_of_t(i):
        part = slice(i * CS, (i + 1) * CS)
        tt[part, :] = nn(rown_t[part, :], yt[...])

    arrive(g_spread.y_in)
    begin(g_spread.x)
    pour(POUR[3])
    rows_of_t(0)
    tt[0:HALF, :] = tt[0:HALF, :] + tn(rq_in[...], edge[1])
    arrive(u_spread.far_in)
    begin(u_spread.y)
    rows_of_t(1)
    rows_of_t(2)
    outgoing.append(pltpu.make_async_copy(tt, t_out, outs.at[0]))
    outgoing[-1].start()

    arrive(g_spread.x_in)
    gp[...] = gbuf[...].reshape(K, K).T
    outgoing.append(pltpu.make_async_copy(gp, gp_out, outs.at[1]))
    outgoing[-1].start()
    eye = iota((K, K), 0) == iota((K, K), 1)
    shifts = jnp.exp(-2.0 * coupling * field[...].astype(f32)) - 1.0
    pair = gp[...]
    diagonal = jnp.sum(jnp.where(eye, pair, 0.0), axis=0, keepdims=True)
    ratio = shifts / (1.0 + (1.0 - diagonal) * shifts)
    ratio_col = jnp.sum(jnp.where(eye, jnp.broadcast_to(ratio, (K, K)), 0.0), axis=1, keepdims=True)
    powers[0] = jnp.where(eye, 0.0, pair * ratio)
    for step in range(3):
        powers[step + 1] = nn(powers[step], powers[step])
    arrive(u_spread.y_in)
    begin(u_spread.x)
    arrive(rows_in)
    rows_twin.start()
    total = jnp.sum(jnp.sum(powers[3] * powers[3], axis=1, keepdims=True), axis=0, keepdims=True)
    norm[...] = jnp.broadcast_to(total, norm.shape)
    outgoing.append(pltpu.make_async_copy(norm, norm_out, outs.at[2]))
    outgoing[-1].start()

    rows_twin_in.wait_recv()
    for k in range(ROWS):
        vall[k * KR : (k + 1) * KR, :] = vbuf[k % 2, k // 2]
    outgoing.append(pltpu.make_async_copy(vall, v_out, outs.at[3]))
    outgoing[-1].start()
    z = vall[...]
    for step in range(4):
        z = z + nn(powers[step], z)
    ws[...] = jnp.zeros_like(ws)
    ws[:, 0:WIDTH] = ratio_col * z
    wt = ws[...].T
    arrive(u_spread.x_in)
    outgoing.append(pltpu.make_async_copy(ubuf, u_out, outs.at[4]))
    outgoing[-1].start()
    for i in range(3):
        part = slice(i * CS, (i + 1) * CS)
        acc[part, :] = tt[part, :] - nn(wt[part, :], ubuf[...].reshape(K, HEIGHT))
        outgoing.append(pltpu.make_async_copy(acc.at[part], acc_out.at[part], outs.at[5 + i]))
        outgoing[-1].start()

    for copy in outgoing:
        copy.wait()
    for copy in near + far + pieces + [pieces_twin] + rows_out + [rows_twin] + u_spread.sent + g_spread.y + g_spread.x:
        copy.wait_send()
    for copy in halos:
        copy.wait()


def finish_kernel(norm_hbm, acc_hbm, halo_hbm, mix_hbm, field_hbm, t_hbm, u_hbm, v_hbm, gp_hbm, out_hbm, norm, acc, halo, mix, field, t, u, v, gp, sem, out_sem):
    first, inner, final = pl.ds(0, HALF), pl.ds(HALF, WIDTH - 2 * HALF), pl.ds(WIDTH - HALF, HALF)
    pairs = [(halo_hbm, halo), (mix_hbm, mix)] + [(acc_hbm.at[part], acc.at[part]) for part in (final, first, inner)]
    pairs.append((norm_hbm, norm))
    loads = [pltpu.make_async_copy(src, dst, sem.at[i]) for i, (src, dst) in enumerate(pairs)]
    stores = [pltpu.make_async_copy(acc.at[part], out_hbm.at[part], out_sem.at[i]) for i, part in enumerate((final, first, inner))]
    for load in loads:
        load.start()
    loads[0].wait()
    loads[1].wait()
    above = tn(mix[...], halo[1])
    loads[2].wait()
    acc[WIDTH - HALF : WIDTH, :] = acc[WIDTH - HALF : WIDTH, :] + above
    stores[0].start()
    loads[3].wait()
    acc[0:HALF, :] = acc[0:HALF, :] + halo[0]
    stores[1].start()
    loads[4].wait()
    stores[2].start()
    loads[5].wait()
    for copy in stores:
        copy.wait()

    @pl.when(jnp.logical_not(norm[0, 0] < series_bound))
    def _():
        for i, (src, dst) in enumerate(((t_hbm, t), (u_hbm, u), (v_hbm, v), (gp_hbm, gp), (field_hbm, field))):
            copy = pltpu.make_async_copy(src, dst, sem.at[i])
            copy.start()
            copy.wait()
        eye = iota((K, K), 0) == iota((K, K), 1)
        ident = jnp.where(eye, 1.0, 0.0)
        shifts = jnp.exp(-2.0 * coupling * field[...].astype(f32)) - 1.0
        gp[...] = ident + (ident - gp[...]) * shifts
        index = iota((K, 1), 0)

        def eliminate(k, carry):
            a = gp[...]
            column = jnp.sum(jnp.where(iota((K, K), 1) == k, a, 0.0), axis=1, keepdims=True)
            size = jnp.where(index >= k, jnp.abs(column), -1.0)
            best = jnp.min(jnp.where(size == jnp.max(size), index, K - 1))
            at_k = jnp.sum(jnp.where(index == k, column, 0.0))
            at_best = jnp.sum(jnp.where(index == best, column, 0.0))
            factors = jnp.where(index == best, at_k, column)
            for ref in (gp, v):
                line = ref[pl.ds(best, 1), :] / at_best
                ref[pl.ds(best, 1), :] = ref[pl.ds(k, 1), :]
                ref[...] = jnp.where(index == k, line, ref[...] - factors * line)
            return carry

        lax.fori_loop(0, K, eliminate, 0)
        shift_col = jnp.sum(jnp.where(eye, jnp.broadcast_to(shifts, (K, K)), 0.0), axis=1, keepdims=True)
        t[...] = t[...] - tn(shift_col * v[...], u[...], highest)
        t[0:HALF, :] = t[0:HALF, :] + halo[0]
        t[WIDTH - HALF : WIDTH, :] = t[WIDTH - HALF : WIDTH, :] + above
        copy = pltpu.make_async_copy(t, out_hbm, sem.at[0])
        copy.start()
        copy.wait()


def on_device(greens, accepted_sites, field_values, left_a, left_b, right_a, right_b):
    hbm = pl.BlockSpec(memory_space=pltpu.HBM)
    shape = lambda *dims: jax.ShapeDtypeStruct(dims, f32)
    v = lambda *dims: pltpu.VMEM(dims, f32)
    dma = lambda *dims: pltpu.SemaphoreType.DMA(dims)
    smem_v = lambda *dims: pltpu.SMEM(dims, jnp.int32)
    field = field_values.reshape(1, K)
    acc, halo, norm, mix, t, u, vv, gp = pl.pallas_call(
        exchange_kernel,
        name="exchange",
        out_shape=[
            shape(WIDTH, HEIGHT), shape(2, HALF, HEIGHT), shape(8, 128), shape(HALF, HALF),
            shape(WIDTH, HEIGHT), shape(COLS, KC, HEIGHT), shape(K, WIDTH), shape(K, K),
        ],
        in_specs=[hbm] * 7,
        out_specs=[hbm] * 8,
        scratch_shapes=[
            smem_v(K), pltpu.VMEM((1, K), jnp.int32), v(WIDTH, HEIGHT), v(6, CS, CS), v(6, CS, CS), v(3, CS, CS), v(3, CS, CS),
            v(WIDTH, HEIGHT), v(WIDTH, HEIGHT), v(WIDTH, HEIGHT), v(HEIGHT, TALL), v(HEIGHT, TALL), v(WIDTH, 128),
            v(HALF, WIDTH), v(HALF, WIDTH), v(2, HALF, WIDTH), v(HALF, HALF), v(HALF, HALF), v(HALF, HALF), v(HALF, HALF),
            v(2, WIDTH, 128), v(2, HALF, WIDTH), v(HALF, WIDE), v(WIDTH, WIDE), v(WIDTH, WIDE), v(WIDTH, WIDTH),
            v(2, KR, 128), v(2, KR, 128), v(2, HALF, HEIGHT), v(2, ROWS, KC, 128), v(COLS, KC, HEIGHT), v(2, 8, KR, WIDTH), v(K, WIDTH),
            v(COLS, KC, K), v(K, K), v(4, K, K), v(K, WIDE), v(8, 128), v(HALF, HALF),
            dma(2, CHUNKS), dma(2, CHUNKS), dma(6), dma(6), dma(16), dma(17), dma(8), dma(9),
            dma(7), dma(7), dma(7), dma(7), dma(7), dma(9),
        ],
        compiler_params=pltpu.CompilerParams(collective_id=0, has_side_effects=True, vmem_limit_bytes=60 * 2**20),
    )(accepted_sites, field, greens.T, left_a, left_b, right_a, right_b)
    out = pl.pallas_call(
        finish_kernel,
        name="finish",
        out_shape=shape(WIDTH, HEIGHT),
        in_specs=[hbm] * 9,
        out_specs=hbm,
        scratch_shapes=[
            pltpu.SMEM((8, 128), f32), v(WIDTH, HEIGHT), v(2, HALF, HEIGHT), v(HALF, HALF), pltpu.VMEM((1, K), jnp.int32),
            v(WIDTH, HEIGHT), v(K, HEIGHT), v(K, WIDTH), v(K, K), dma(6), dma(3),
        ],
        compiler_params=pltpu.CompilerParams(vmem_limit_bytes=60 * 2**20),
    )(norm, acc, halo, mix, field, t, u.reshape(K, HEIGHT), vv, gp)
    return out.T


def solution(mesh):
    return jax.shard_map(
        on_device,
        mesh=mesh,
        in_specs=(
            P("row", "col"),
            P(),
            P(),
            P("row", None, None),
            P("row", None, None),
            P("col", None, None),
            P("col", None, None),
        ),
        out_specs=P("row", "col"),
        check_vma=False,
    )
```

time: 146 us -> 97.3 us (0.67)
  the two profiles are of different devices: /device:TPU:3 before, /device:TPU:88 now
where the time goes in v3:
time: 97.3 us; the launch traced here: 97.1 us
  Pallas kernels  96.9 us (100%)
    pallas_call x1, Pallas kernels, on_device(): pl.pallas_call(exchange_kernel, name='exchange', out_shape=[shape(WIDTH,...  94.4 us
    pallas_call x1, Pallas kernels, on_device(): pl.pallas_call(finish_kernel, name='finish', out_shape=shape(WIDTH, HEIGH...  2.6 us

profile of v3, /device:TPU:88, one launch (start us, length us, event | category | flops | bytes accessed | tf_op | source)
XLA Modules:
  0.0 97.1 jit_solution(10357914270778990641)
XLA Ops:
  0.0 94.4 %exchange.1 = (f32[432,864]{1,0:T(8,128)}, f32[2,72,864]{2,1,0:T(8,128)}, f32[8,128]{1,0:T(8,128)}, f32[72,72]{1,0:T(8,128)}, f32[432,864]{1,0:T(8,128)}, /*inde...) custom-call(s32[256]{0:T(256)} %sites_hbm.1, s32[1,256]{1,0:T(1,128)} %bitcast.6, f32[432,864]{1,0:T(8,128)} %bitcast.4, ...), custom_call_target="tpu_custom_call" | custom-call | tf_op jit(solution)/shard_map/exchange/pallas_call | solution.py:374
  94.4 2.6 %finish.1 = f32[432,864]{1,0:T(8,128)} custom-call(f32[8,128]{1,0:T(8,128)} %get-tuple-element.13.norm_hbm, f32[432,864]{1,0:T(8,128)} %get-tuple-element.14.acc_hbm, f32[2,72,864]{2,1,0:T(8,128)} %get-tuple-element.15.halo_hbm, f32[72,72]{1,0:T(8,128)} %get-tuple-element.16.mix_hbm, s32[1,256]{1,0:T(1,128)} %bitcast.7, f32[432,864]{1,0:T(8,128)} %get-tuple-element.17.t_hbm, ...), custom_call_target="tpu_custom_call" | custom-call | tf_op jit(solution)/shard_map/finish/pallas_call | solution.py:395

commit v4 on v3

--- a/solution.py
+++ b/solution.py
@@ -21,8 +21,6 @@
 WIDE = 512
 TALL = 896
 BANDS = ((0, 256, 0, 512), (256, 512, 128, 768), (512, 768, 384, HEIGHT), (768, HEIGHT, 512, HEIGHT))
-CHUNKS = 9
-POUR = (9, 0, 0, 9)
 
 
 def dot(a, b, da, db, precision):
@@ -180,10 +178,9 @@
     right = nn(x, rown[...])
     for a, b, lo, hi in BANDS:
         yt[:, a:b] = nt(gt[:, lo:hi], lf[a:b, lo:hi])
-    arrive(far)
-    first = x_in[0] + jnp.concatenate([nn(xs[1][:, 0:HALF], rq_in[...]), jnp.zeros((KR, 128 - HALF), f32)], axis=1)
+    arrive(far[0:2])
     right += nn(x_in[1][:, 0:HALF], wd[...])
-    vbuf[core, zl] = right[:, 0:WIDTH] + jnp.concatenate([first, jnp.zeros((KR, WIDTH - 128), f32)], axis=1)
+    vbuf[core, zl] = right + jnp.concatenate([x_in[0], jnp.zeros((KR, 256), f32), pltpu.roll(xs[1], 48, 1)], axis=1)
     begin(rows_out)
     arrive(near)
     one = jnp.where(iota((HALF, HALF), 0) == iota((HALF, HALF), 1), 1.0, 0.0)
@@ -193,17 +190,7 @@
 
     edge[0] = nn(redge_t[0, :, 256:WIDTH], yt[256:WIDTH, :])
     edge[1] = nn(redge_t[1, :, 0:CS], yt[0:CS, :])
-    halos = []
-    for k in range(CHUNKS):
-        part = pl.ds(k * 8, 8)
-        for d, to in ((0, cup), (1, cdn)):
-            halos.append(remote(edge.at[d, part], halo_out.at[d, part], es.at[d, k], er.at[d, k], (r, to)))
-    poured = [0]
-
-    def pour(n):
-        begin(halos[poured[0] * 2 : (poured[0] + n) * 2])
-        poured[0] = min(poured[0] + n, CHUNKS)
-
+    halos = [remote(edge.at[d], halo_out.at[d], es.at[d], er.at[d], (r, to)) for d, to in ((0, cup), (1, cdn))]
     class Spread:
         def __init__(self, buf, send, recv):
             def go(first, count, i, to):
@@ -221,11 +208,10 @@
     u_spread, g_spread = Spread(ubuf, us, ur), Spread(gbuf, gs, gr)
     ubuf[c] = site_rows(yt)
     begin(u_spread.far)
-    pour(POUR[0])
+    begin(halos)
 
     arrive(pieces_in)
     pieces_twin.start()
-    pour(POUR[1])
     pieces_twin_in.wait_recv()
     for side in (0, 1):
         halves = []
@@ -236,7 +222,6 @@
             halves.append(half)
         gbuf[xy * 2 + side] = jnp.concatenate(halves, axis=1)
     begin(g_spread.y)
-    pour(POUR[2])
     rown_t[...] = rown[...].T[0:WIDTH, :]
 
     def rows_of_t(i):
@@ -245,7 +230,7 @@
 
     arrive(g_spread.y_in)
     begin(g_spread.x)
-    pour(POUR[3])
+    far[2].wait_recv()
     rows_of_t(0)
     tt[0:HALF, :] = tt[0:HALF, :] + tn(rq_in[...], edge[1])
     arrive(u_spread.far_in)
@@ -280,9 +265,11 @@
     rows_twin_in.wait_recv()
     for k in range(ROWS):
         vall[k * KR : (k + 1) * KR, :] = vbuf[k % 2, k // 2]
+    met = nn(pltpu.roll(vall[:, 384:WIDE], 80, 1)[:, 0:HALF], rq_in[...])
+    vall[:, 0:HALF] = vall[:, 0:HALF] + met
     outgoing.append(pltpu.make_async_copy(vall, v_out, outs.at[3]))
     outgoing[-1].start()
-    z = vall[...]
+    z = vall[:, 0:WIDTH]
     for step in range(4):
         z = z + nn(powers[step], z)
     ws[...] = jnp.zeros_like(ws)
@@ -356,7 +343,7 @@
 
         lax.fori_loop(0, K, eliminate, 0)
         shift_col = jnp.sum(jnp.where(eye, jnp.broadcast_to(shifts, (K, K)), 0.0), axis=1, keepdims=True)
-        t[...] = t[...] - tn(shift_col * v[...], u[...], highest)
+        t[...] = t[...] - tn(shift_col * v[:, 0:WIDTH], u[...], highest)
         t[0:HALF, :] = t[0:HALF, :] + halo[0]
         t[WIDTH - HALF : WIDTH, :] = t[WIDTH - HALF : WIDTH, :] + above
         copy = pltpu.make_async_copy(t, out_hbm, sem.at[0])
@@ -376,7 +363,7 @@
         name="exchange",
         out_shape=[
             shape(WIDTH, HEIGHT), shape(2, HALF, HEIGHT), shape(8, 128), shape(HALF, HALF),
-            shape(WIDTH, HEIGHT), shape(COLS, KC, HEIGHT), shape(K, WIDTH), shape(K, K),
+            shape(WIDTH, HEIGHT), shape(COLS, KC, HEIGHT), shape(K, WIDE), shape(K, K),
         ],
         in_specs=[hbm] * 7,
         out_specs=[hbm] * 8,
@@ -385,9 +372,9 @@
             v(WIDTH, HEIGHT), v(WIDTH, HEIGHT), v(WIDTH, HEIGHT), v(HEIGHT, TALL), v(HEIGHT, TALL), v(WIDTH, 128),
             v(HALF, WIDTH), v(HALF, WIDTH), v(2, HALF, WIDTH), v(HALF, HALF), v(HALF, HALF), v(HALF, HALF), v(HALF, HALF),
             v(2, WIDTH, 128), v(2, HALF, WIDTH), v(HALF, WIDE), v(WIDTH, WIDE), v(WIDTH, WIDE), v(WIDTH, WIDTH),
-            v(2, KR, 128), v(2, KR, 128), v(2, HALF, HEIGHT), v(2, ROWS, KC, 128), v(COLS, KC, HEIGHT), v(2, 8, KR, WIDTH), v(K, WIDTH),
+            v(2, KR, 128), v(2, KR, 128), v(2, HALF, HEIGHT), v(2, ROWS, KC, 128), v(COLS, KC, HEIGHT), v(2, 8, KR, WIDE), v(K, WIDE),
             v(COLS, KC, K), v(K, K), v(4, K, K), v(K, WIDE), v(8, 128), v(HALF, HALF),
-            dma(2, CHUNKS), dma(2, CHUNKS), dma(6), dma(6), dma(16), dma(17), dma(8), dma(9),
+            dma(2), dma(2), dma(6), dma(6), dma(16), dma(17), dma(8), dma(9),
             dma(7), dma(7), dma(7), dma(7), dma(7), dma(9),
         ],
         compiler_params=pltpu.CompilerParams(collective_id=0, has_side_effects=True, vmem_limit_bytes=60 * 2**20),
@@ -400,7 +387,7 @@
         out_specs=hbm,
         scratch_shapes=[
             pltpu.SMEM((8, 128), f32), v(WIDTH, HEIGHT), v(2, HALF, HEIGHT), v(HALF, HALF), pltpu.VMEM((1, K), jnp.int32),
-            v(WIDTH, HEIGHT), v(K, HEIGHT), v(K, WIDTH), v(K, K), dma(6), dma(3),
+            v(WIDTH, HEIGHT), v(K, HEIGHT), v(K, WIDE), v(K, K), dma(6), dma(3),
         ],
         compiler_params=pltpu.CompilerParams(vmem_limit_bytes=60 * 2**20),
     )(norm, acc, halo, mix, field, t, u.reshape(K, HEIGHT), vv, gp)

time: 97.3 us -> 92.7 us (0.953)
  the two profiles are of different devices: /device:TPU:88 before, /device:TPU:120 now
where the time goes in v4:
time: 92.7 us; the launch traced here: 92.6 us
  Pallas kernels  92.4 us (100%)
    pallas_call x1, Pallas kernels, on_device(): pl.pallas_call(exchange_kernel, name='exchange', out_shape=[shape(WIDTH,...  89.8 us
    pallas_call x1, Pallas kernels, on_device(): pl.pallas_call(finish_kernel, name='finish', out_shape=shape(WIDTH, HEIGH...  2.6 us

profile of v4, /device:TPU:120, one launch (start us, length us, event | category | flops | bytes accessed | tf_op | source)
XLA Modules:
  0.0 92.6 jit_solution(10493332406789775580)
XLA Ops:
  0.0 89.8 %exchange.1 = (f32[432,864]{1,0:T(8,128)}, f32[2,72,864]{2,1,0:T(8,128)}, f32[8,128]{1,0:T(8,128)}, f32[72,72]{1,0:T(8,128)}, f32[432,864]{1,0:T(8,128)}, /*inde...) custom-call(s32[256]{0:T(256)} %sites_hbm.1, s32[1,256]{1,0:T(1,128)} %bitcast.6, f32[432,864]{1,0:T(8,128)} %bitcast.4, ...), custom_call_target="tpu_custom_call" | custom-call | tf_op jit(solution)/shard_map/exchange/pallas_call | solution.py:361
  89.8 2.6 %finish.1 = f32[432,864]{1,0:T(8,128)} custom-call(f32[8,128]{1,0:T(8,128)} %get-tuple-element.13.norm_hbm, f32[432,864]{1,0:T(8,128)} %get-tuple-element.14.acc_hbm, f32[2,72,864]{2,1,0:T(8,128)} %get-tuple-element.15.halo_hbm, f32[72,72]{1,0:T(8,128)} %get-tuple-element.16.mix_hbm, s32[1,256]{1,0:T(1,128)} %bitcast.7, f32[432,864]{1,0:T(8,128)} %get-tuple-element.17.t_hbm, ...), custom_call_target="tpu_custom_call" | custom-call | tf_op jit(solution)/shard_map/finish/pallas_call | solution.py:382

commit v5 on v4

--- a/solution.py
+++ b/solution.py
@@ -46,7 +46,7 @@
 def exchange_kernel(
     sites_hbm, field_hbm, gt_hbm, la_hbm, lb_hbm, ra_hbm, rb_hbm,
     acc_out, halo_out, norm_out, mix_out, t_out, u_out, v_out, gp_out,
-    sites, field, gt, la, lb, ra, rb, yt, tt, acc, ma, lf, rt, qtop, pbot, top_in, lq_s, lq_in, rq_s, rq_in, redge, redge_t, wd, bloc, rown, rown_t,
+    sites, field, gt, la, lb, ra, rb, yt, tt, acc, ma, lf, rt, qtop, pbot, top_in, rq_s, rq_in, redge, redge_t, wd, bloc, rown, rown_t,
     xs, x_in, edge, pbuf, ubuf, vbuf, vall, gbuf, gp, powers, ws, norm, mix,
     es, er, ns, nr, ps, pr, vs, vr, us, ur, gs, gr, ins, outs,
 ):
@@ -141,18 +141,19 @@
     loads[4].wait()
     loads[5].wait()
     loads[6].wait()
-    lq_s[...] = lb[5][HALF:CS, HALF:CS]
+    pbot[...] = jnp.zeros_like(pbot)
+    qtop[...] = jnp.zeros_like(qtop)
+    pbot[:, WIDTH : WIDTH + HALF] = lb[5][HALF:CS, HALF:CS]
 
     for i in range(6):
         ma[i * CS : (i + 1) * CS, i * CS : (i + 1) * CS] = la[i]
-    qtop[...] = nt(la[0, 0:HALF, :], gt[:, 0:CS])
+    qtop[:, 0:WIDTH] = nt(la[0, 0:HALF, :], gt[:, 0:CS])
     last = nn(lb[5][HALF:CS, 0:HALF], ma[HEIGHT - HALF : HEIGHT, 640:TALL], highest)
-    pbot[...] = nt(last[:, 0 : HEIGHT - 640], gt[:, 640:HEIGHT])
+    pbot[:, 0:WIDTH] = nt(last[:, 0 : HEIGHT - 640], gt[:, 640:HEIGHT])
 
     near = [
         remote(pbot, top_in.at[0], ns.at[0], nr.at[0], (rup, c)),
         remote(qtop, top_in.at[1], ns.at[1], nr.at[1], (rdn, c)),
-        remote(lq_s, lq_in, ns.at[2], nr.at[2], (rup, c)),
     ]
     begin(near)
 
@@ -184,9 +185,9 @@
     begin(rows_out)
     arrive(near)
     one = jnp.where(iota((HALF, HALF), 0) == iota((HALF, HALF), 1), 1.0, 0.0)
-    yt[:, 0:HALF] = tn(jnp.concatenate([top_in[0], nn(lq_in[...], qtop[...])], axis=0), jnp.concatenate([one, one], axis=0))
+    yt[:, 0:HALF] = tn(jnp.concatenate([top_in[0, :, 0:WIDTH], nn(pltpu.roll(top_in[0, :, 384:WIDE], 80, 1)[:, 0:HALF], qtop[:, 0:WIDTH])], axis=0), jnp.concatenate([one, one], axis=0))
     tail = jnp.concatenate([jnp.zeros((24, HALF), f32), lb[5][0:HALF, HALF:CS]], axis=0)
-    yt[:, 768:HEIGHT] = yt[:, 768:HEIGHT] + tn(top_in[1], tail.T)
+    yt[:, 768:HEIGHT] = yt[:, 768:HEIGHT] + tn(top_in[1, :, 0:WIDTH], tail.T)
 
     edge[0] = nn(redge_t[0, :, 256:WIDTH], yt[256:WIDTH, :])
     edge[1] = nn(redge_t[1, :, 0:CS], yt[0:CS, :])
@@ -370,7 +371,7 @@
         scratch_shapes=[
             smem_v(K), pltpu.VMEM((1, K), jnp.int32), v(WIDTH, HEIGHT), v(6, CS, CS), v(6, CS, CS), v(3, CS, CS), v(3, CS, CS),
             v(WIDTH, HEIGHT), v(WIDTH, HEIGHT), v(WIDTH, HEIGHT), v(HEIGHT, TALL), v(HEIGHT, TALL), v(WIDTH, 128),
-            v(HALF, WIDTH), v(HALF, WIDTH), v(2, HALF, WIDTH), v(HALF, HALF), v(HALF, HALF), v(HALF, HALF), v(HALF, HALF),
+            v(HALF, WIDE), v(HALF, WIDE), v(2, HALF, WIDE), v(HALF, HALF), v(HALF, HALF),
             v(2, WIDTH, 128), v(2, HALF, WIDTH), v(HALF, WIDE), v(WIDTH, WIDE), v(WIDTH, WIDE), v(WIDTH, WIDTH),
             v(2, KR, 128), v(2, KR, 128), v(2, HALF, HEIGHT), v(2, ROWS, KC, 128), v(COLS, KC, HEIGHT), v(2, 8, KR, WIDE), v(K, WIDE),
             v(COLS, KC, K), v(K, K), v(4, K, K), v(K, WIDE), v(8, 128), v(HALF, HALF),

time: 92.7 us -> 95.2 us (1.027)
  the two profiles are of different devices: /device:TPU:120 before, /device:TPU:64 now
where the time goes in v5:
time: 95.2 us; the launch traced here: 95 us
  Pallas kernels  94.9 us (100%)
    pallas_call x1, Pallas kernels, on_device(): pl.pallas_call(exchange_kernel, name='exchange', out_shape=[shape(WIDTH,...  92.3 us
    pallas_call x1, Pallas kernels, on_device(): pl.pallas_call(finish_kernel, name='finish', out_shape=shape(WIDTH, HEIGH...  2.6 us

profile of v5, /device:TPU:64, one launch (start us, length us, event | category | flops | bytes accessed | tf_op | source)
XLA Modules:
  0.0 95.0 jit_solution(11213103261863346422)
XLA Ops:
  0.0 92.3 %exchange.1 = (f32[432,864]{1,0:T(8,128)}, f32[2,72,864]{2,1,0:T(8,128)}, f32[8,128]{1,0:T(8,128)}, f32[72,72]{1,0:T(8,128)}, f32[432,864]{1,0:T(8,128)}, /*inde...) custom-call(s32[256]{0:T(256)} %sites_hbm.1, s32[1,256]{1,0:T(1,128)} %bitcast.6, f32[432,864]{1,0:T(8,128)} %bitcast.4, ...), custom_call_target="tpu_custom_call" | custom-call | tf_op jit(solution)/shard_map/exchange/pallas_call | solution.py:362
  92.3 2.6 %finish.1 = f32[432,864]{1,0:T(8,128)} custom-call(f32[8,128]{1,0:T(8,128)} %get-tuple-element.13.norm_hbm, f32[432,864]{1,0:T(8,128)} %get-tuple-element.14.acc_hbm, f32[2,72,864]{2,1,0:T(8,128)} %get-tuple-element.15.halo_hbm, f32[72,72]{1,0:T(8,128)} %get-tuple-element.16.mix_hbm, s32[1,256]{1,0:T(1,128)} %bitcast.7, f32[432,864]{1,0:T(8,128)} %get-tuple-element.17.t_hbm, ...), custom_call_target="tpu_custom_call" | custom-call | tf_op jit(solution)/shard_map/finish/pallas_call | solution.py:383
